TPU v7x, 32 devices: a whole 2x2x4 slice. The times are simulated.
32 devices in a mesh: task: 4 (over y, x), batch: 8 (over z, core).
Axes of the slice: x: 2, y: 2, z: 4, core: 2. Of those that a mesh axis runs over, the one named last changes fastest.
Arguments:
- images: bfloat16 [32, 18, 24, 512], P(('task', 'batch')), may hold values from -6 to 6
- image_small: int32 [32], P(('task', 'batch')), may hold values from 0 to 1, as said below
- pool_index: int32 [32, 9, 12], P(('task', 'batch')), may hold values from 0 to 3
- row_slot: int32 [9216], replicated, may hold values from 0 to 9215, each once
- trunk_weight: float32 [9216, 512], P('batch'), may hold values from -0.09375 to 0.09375
- trunk_mean_grad: float32 [9216, 512], P('batch'), may hold values from -5.173322 to 5.173322
- trunk_mean_square: float32 [9216, 512], P('batch'), may hold values from 7.32672 to 116.1216
- trunk_statistic: float32 [2, 512, 512], replicated, as said below
- trunk_basis: float32 [2, 512, 512], replicated, as said below
- head_weight: float32 [4, 5632, 512], P('task', 'batch'), may hold values from -0.15625 to 0.15625
- head_mean_grad: float32 [4, 5632, 512], P('task', 'batch'), may hold values from -5.173322 to 5.173322
- head_mean_square: float32 [4, 5632, 512], P('task', 'batch'), may hold values from 7.32672 to 116.1216
- head_statistic: float32 [4, 3, 512, 512], P('task'), as said below
- head_basis: float32 [4, 3, 512, 512], P('task'), as said below
- trunk_gain: float32 [2, 512], replicated, may hold values from 0.5 to 1.5
- trunk_offset: float32 [2, 512], replicated, may hold values from -1.2 to 1.2
- trunk_norm_mean_grad: float32 [2, 2, 512], replicated, may hold values from -5.173322 to 5.173322
- trunk_norm_mean_square: float32 [2, 2, 512], replicated, may hold values from 7.32672 to 116.1216
- head_gain: float32 [4, 3, 512], P('task'), may hold values from 0.5 to 1.5
- head_offset: float32 [4, 3, 512], P('task'), may hold values from -1.2 to 1.2
- head_norm_mean_grad: float32 [4, 3, 2, 512], P('task'), may hold values from -5.173322 to 5.173322
- head_norm_mean_square: float32 [4, 3, 2, 512], P('task'), may hold values from 7.32672 to 116.1216
- cotangent: bfloat16 [4, 4, 8, 9, 12, 512], P('task', None, 'batch'), may hold values from -6 to 6
Outputs:
- task_features: bfloat16 [4, 4, 8, 9, 12, 512], P('task', None, 'batch')
- input_grad: float32 [32, 18, 24, 512], P(('task', 'batch'))
- trunk_weight_new: float32 [9216, 512], P('batch')
- trunk_mean_grad_new: float32 [9216, 512], P('batch')
- trunk_mean_square_new: float32 [9216, 512], P('batch')
- trunk_statistic_new: float32 [2, 512, 512], replicated
- trunk_basis_new: float32 [2, 512, 512], replicated
- head_weight_new: float32 [4, 5632, 512], P('task', 'batch')
- head_mean_grad_new: float32 [4, 5632, 512], P('task', 'batch')
- head_mean_square_new: float32 [4, 5632, 512], P('task', 'batch')
- head_statistic_new: float32 [4, 3, 512, 512], P('task')
- head_basis_new: float32 [4, 3, 512, 512], P('task')
- trunk_norm_new: float32 [2, 2, 512], replicated
- trunk_norm_mean_grad_new: float32 [2, 2, 512], replicated
- trunk_norm_mean_square_new: float32 [2, 2, 512], replicated
- head_norm_new: float32 [4, 3, 2, 512], P('task')
- head_norm_mean_grad_new: float32 [4, 3, 2, 512], P('task')
- head_norm_mean_square_new: float32 [4, 3, 2, 512], P('task')
Inputs may be any that keep to these rules, and one draw needn't show every extreme that they name: `image_small`: 1 marks a 144x192 image whose valid region is its first 9 rows and 12 columns; 0 marks a 288x384 image, valid everywhere. `pool_index`: which cell of a 2x2 window receives the value: 2 times the row offset plus the column offset. A permutation: row r of the stacked trunk kernels is held at row row_slot[r] of the slot-ordered arrays. `trunk_statistic`: each matrix is symmetric with a dominant positive diagonal. `head_statistic`: each matrix is symmetric with a dominant positive diagonal. `trunk_basis`: each matrix is orthogonal. `head_basis`: each matrix is orthogonal.
All inputs are finite; a program needn't handle non-finite values.
Results may differ from a plain program's by a relative error of at most 0.023.
Values may be sent and summed in bfloat16 or wider, within the bound.
A program may use at most 320 MiB of HBM per device.

v0:
```python
import functools

import jax
import jax.numpy as jnp
from jax import lax
from jax.experimental import pallas as pl
from jax.experimental.pallas import tpu as pltpu
from jax.sharding import PartitionSpec as P

STEP = 10


EPS = 1e-05
ADAM_EPS = 1e-08
BETA_ONE = 0.95
BETA_TWO = 0.95
STAT_DECAY = 0.95
LEARN_MATRIX = 0.02
LEARN_NORM = 0.5
DECAY_MATRIX = 0.01
BF = jnp.bfloat16
F32 = jnp.float32
MESH = pl.DeviceIdType.MESH
MIB = 1 << 20

VMEM_SPEC = pl.BlockSpec(memory_space=pltpu.VMEM)
SMEM_SPEC = pl.BlockSpec(memory_space=pltpu.SMEM)


def run(body, outs, specs, args, scratch=(), vmem=40, flops=0):
    size = sum(o.size * o.dtype.itemsize for o in outs) + sum(a.size * a.dtype.itemsize for a in args)
    return pl.pallas_call(
        body,
        out_shape=tuple(outs),
        in_specs=[SMEM_SPEC if s == "s" else VMEM_SPEC for s in specs],
        out_specs=tuple(VMEM_SPEC for _ in outs),
        scratch_shapes=list(scratch),
        compiler_params=pltpu.CompilerParams(vmem_limit_bytes=vmem * MIB),
        cost_estimate=pl.CostEstimate(flops=flops, bytes_accessed=size, transcendentals=0),
    )(*args)


def shape(dims, kind):
    return jax.ShapeDtypeStruct(tuple(dims), kind)


def dot(a, b):
    return jnp.dot(a, b, preferred_element_type=F32)


def dot_nt(a, b):
    return lax.dot_general(a, b, (((1,), (1,)), ((), ())), preferred_element_type=F32)


def dot_tn(a, b):
    return lax.dot_general(a, b, (((0,), (0,)), ((), ())), preferred_element_type=F32)


def split(a):
    high = a.astype(BF)
    return high, (a - high.astype(F32)).astype(BF)


def dot3(kind, a, b):
    dims = {dot: (1, 0), dot_nt: (1, 1), dot_tn: (0, 0)}[kind]
    a_high, a_low = split(a)
    b_high, b_low = split(b)
    return kind(
        jnp.concatenate([a_high, a_high, a_low], axis=dims[0]),
        jnp.concatenate([b_high, b_low, b_high], axis=dims[1]),
    )


def places(height, breadth):
    index = lax.broadcasted_iota(jnp.int32, (height * breadth, 1), 0)
    row = lax.div(index, breadth)
    return row, index - row * breadth


def valid_rows(small, height, breadth):
    row, col = places(height, breadth)
    row_limit = jnp.where(small > 0, height // 2, height)
    col_limit = jnp.where(small > 0, breadth // 2, breadth)
    return jnp.where((row < row_limit) & (col < col_limit), 1.0, 0.0).astype(F32)


def move(values, rows):
    gap = jnp.zeros((abs(rows),) + values.shape[1:], values.dtype)
    if rows > 0:
        return jnp.concatenate([gap, values[:-rows]], axis=0)
    return jnp.concatenate([values[-rows:], gap], axis=0)


def from_left(values, col):
    return jnp.where(col > 0, pltpu.roll(values, 1, 0), 0.0)


def from_right(values, col, breadth):
    return jnp.where(col < breadth - 1, pltpu.roll(values, values.shape[0] - 1, 0), 0.0)


def gather_taps(tap, breadth, col):
    lines = [move(tap(b), breadth) + tap(3 + b) + move(tap(6 + b), -breadth) for b in range(3)]
    return lines[1] + from_left(lines[0], col) + from_right(lines[2], col, breadth)


def spread_taps(values, breadth, col):
    lines = [from_right(values, col, breadth), values, from_left(values, col)]
    return [
        move(lines[b], breadth * (a - 1)) if a != 1 else lines[b] for a in range(3) for b in range(3)
    ]


def window_sum(values, row, col, breadth):
    count = values.shape[0]
    pair = values + jnp.where(
        col % 2 == 0, pltpu.roll(values, count - 1, 0), pltpu.roll(values, 1, 0)
    )
    return pair + jnp.where(row % 2 == 0, move(pair, -breadth), move(pair, breadth))


def silu_back(scaled):
    sig = jax.nn.sigmoid(scaled)
    return sig * (1.0 + scaled * (1.0 - sig))


def col_sum(values):
    return jnp.sum(values, axis=0, keepdims=True)


def put_sums(ref, rows):
    width = ref.shape[1]
    rows = list(rows) + [jnp.zeros((1, width), F32)] * (8 - len(rows))
    ref[...] = jnp.concatenate(rows, axis=0)


def each_image(geometry, body, start):
    number, height, breadth = geometry
    pixels = height * breadth

    def step(image, carry):
        return body(image, pl.ds(pl.multiple_of(image * pixels, 16), pixels), carry)

    return lax.fori_loop(0, number, step, start)


def zero_rows(count, width):
    return (jnp.zeros((1, width), F32),) * count


def greet(axes):
    barrier = pltpu.get_barrier_semaphore()
    for axis, size in axes:
        me = lax.axis_index(axis)
        for step in range(1, size):
            pl.semaphore_signal(
                barrier, inc=1, device_id={axis: lax.rem(me + step, size)}, device_id_type=MESH
            )
    pl.semaphore_wait(barrier, sum(size - 1 for _, size in axes))


def remote(source, target, sends, receives, peer, axis):
    return pltpu.make_async_remote_copy(
        src_ref=source,
        dst_ref=target,
        send_sem=sends,
        recv_sem=receives,
        device_id={axis: peer},
        device_id_type=MESH,
    )


def pack(rows):
    parts = [row[:, i : i + 128] for row in rows for i in range(0, row.shape[1], 128)]
    parts += [jnp.zeros((1, 128), F32)] * (8 - len(parts))
    return jnp.concatenate(parts, axis=0)


def unpack(tile, count, width):
    per = width // 128
    return [
        jnp.concatenate([tile[k * per + i : k * per + i + 1, :] for i in range(per)], axis=1)
        for k in range(count)
    ]


def total_rows(k, axis, size, rows, mine, slots, sends, receives):
    me = lax.axis_index(axis)
    tile = pack(rows)
    mine[k] = tile
    slots[k, me] = tile
    for step in range(1, size):
        peer = lax.rem(me + step, size)
        remote(mine.at[k], slots.at[k, me], sends.at[k, step], receives.at[k, me], peer, axis).start()
    for step in range(1, size):
        peer = lax.rem(me + size - step, size)
        remote(
            mine.at[k], slots.at[k, peer], sends.at[k, step], receives.at[k, peer], peer, axis
        ).wait_recv()
    total = slots[k, 0]
    for peer in range(1, size):
        total = total + slots[k, peer]
    for step in range(1, size):
        peer = lax.rem(me + step, size)
        remote(
            mine.at[k], slots.at[k, me], sends.at[k, step], receives.at[k, me], peer, axis
        ).wait_send()
    return unpack(total, len(rows), rows[0].shape[1])


def total_scratch(count, size):
    return [
        pltpu.VMEM((count, 8, 128), F32),
        pltpu.VMEM((count, size, 8, 128), F32),
        pltpu.SemaphoreType.DMA((count, size)),
        pltpu.SemaphoreType.DMA((count, size)),
    ]


def columns_of(place, width):
    return pl.ds(pl.multiple_of(place * width, 128), width)


SPECS = {"s": SMEM_SPEC, "v": VMEM_SPEC, "h": pl.BlockSpec(memory_space=pltpu.HBM)}


def exchange_kernel(body, outs, specs, args, scratch, identity, vmem, flops=0, places_out=None):
    size = sum(o.size * o.dtype.itemsize for o in outs) + sum(a.size * a.dtype.itemsize for a in args)
    return pl.pallas_call(
        body,
        out_shape=tuple(outs),
        in_specs=[SPECS[s] for s in specs],
        out_specs=tuple(SPECS[s] for s in places_out or "v" * len(outs)),
        scratch_shapes=list(scratch),
        compiler_params=pltpu.CompilerParams(
            vmem_limit_bytes=vmem * MIB, collective_id=identity, has_side_effects=True
        ),
        cost_estimate=pl.CostEstimate(flops=flops, bytes_accessed=size, transcendentals=0),
    )(*args)


def norm_with(values, totals, scale):
    total, squares, count = totals
    center = total / count
    inverse = lax.rsqrt(squares / count - center * center + EPS)
    normal = (values - center) * inverse
    return normal, inverse, normal * scale[0] + scale[1]


def norm_back_with(upstream, normal, inverse, count, sums, scale, valid):
    return scale[0] * inverse * (upstream - sums[0] / count - normal * (sums[1] / count)) * valid


def silu(values):
    return values * jax.nn.sigmoid(values)


def window_count(height, breadth):
    return -(-(height * breadth // 4) // 16) * 16


def pool_choice(height, breadth, windows, flipped):
    pixels = height * breadth
    dims = (windows, pixels) if flipped else (pixels, windows)
    pixel = lax.broadcasted_iota(jnp.int32, dims, 1 if flipped else 0)
    window = lax.broadcasted_iota(jnp.int32, dims, 0 if flipped else 1)
    row = lax.div(pixel, breadth)
    col = pixel - row * breadth
    home = lax.div(row, 2) * (breadth // 2) + lax.div(col, 2)
    return jnp.where(home == window, 1.0, 0.0).astype(F32)


def rows_of(ref, first, count):
    return [ref[first + k : first + k + 1, :] for k in range(count)]


def window_rows(i, windows):
    return pl.ds(pl.multiple_of(i * windows, 16), windows)


def trunk_forward_body(
    geometry, tasks, batches,
    small, x, enc_taps, dec_taps, scales, choose,
    enc_totals, dec_totals, features, *rest,
):
    kept, (enc_pre, dec_pre, spread), rest = rest[:6], rest[6:9], rest[9:]
    (
        work, pooled, pooled_all, part, pool_sends, pool_receives, sends, receives,
    mine, slots, total_sends, total_receives, saved,
    ) = rest
    number, height, breadth = geometry
    width = enc_pre.shape[1]
    windows = window_count(height, breadth)
    task = lax.axis_index("task")
    _, col = places(height, breadth)
    widen = pool_choice(height, breadth, windows, False).astype(BF)
    narrow = pool_choice(height, breadth, windows, True).astype(BF)

    sources = (x, enc_taps, dec_taps, enc_pre, dec_pre, spread)
    saves = [pltpu.make_async_copy(a, b, saved.at[k]) for k, (a, b) in enumerate(zip(sources, kept))]
    for copy in saves[:3]:
        copy.start()

    def conv(x, taps, pre):
        def image(i, rows, carry):
            valid = valid_rows(small[i], height, breadth)
            work[...] = dot(x[rows, :], taps[...])
            out = gather_taps(lambda p: work[:, p * width : (p + 1) * width], breadth, col)
            pre[rows, :] = out
            kept = out * valid
            return (
                carry[0] + col_sum(kept),
                carry[1] + col_sum(kept * out),
                carry[2] + jnp.broadcast_to(col_sum(valid), (1, width)),
            )

        return each_image(geometry, image, zero_rows(3, width))

    def total(k, rows):
        return total_rows(
            k, "batch", batches, list(rows), mine, slots, total_sends, total_receives
        )

    sums = conv(x, enc_taps, enc_pre)
    saves[3].start()
    greet((("task", tasks), ("batch", batches)))
    totals = total(0, sums)
    put_sums(enc_totals, totals)
    scale = rows_of(scales, 0, 2)

    def peer_of(step, incoming):
        return lax.rem(task + (tasks - step if incoming else step), tasks)

    def pool_copy(i, step, incoming=False):
        rows = window_rows(i, windows)
        peer = peer_of(step, incoming)
        target = pooled_all.at[rows, columns_of(peer if incoming else task, width)]
        return remote(
            pooled.at[rows, :], target, pool_sends.at[i, step], pool_receives.at[i, step], peer, "task"
        )

    def pool(i, rows, carry):
        valid = valid_rows(small[i], height, breadth)
        _, _, scaled = norm_with(enc_pre[rows, :], totals, scale)
        high, low = split(silu(scaled) * valid)
        mean = ((dot(narrow, high) + dot(narrow, low)) * 0.25).astype(BF)
        here = window_rows(i, windows)
        pooled[here, :] = mean
        pooled_all[here, columns_of(task, width)] = mean
        for step in range(1, tasks):
            pool_copy(i, step).start()
        return carry

    each_image(geometry, pool, 0)

    def unpool(i, rows, carry):
        for step in range(1, tasks):
            pool_copy(i, step, True).wait_recv()
        wide = dot(widen, pooled_all[window_rows(i, windows), :])
        spread[rows, :] = (wide * choose[rows, :]).astype(BF)
        return carry

    each_image(geometry, unpool, 0)
    saves[5].start()
    sums = conv(spread, dec_taps, dec_pre)
    saves[4].start()
    totals = total(1, sums)
    put_sums(dec_totals, totals)
    scale = rows_of(scales, 2, 2)

    def feature_copy(i, rows, step, incoming=False):
        peer = peer_of(step, incoming)
        target = features.at[rows, columns_of(peer if incoming else task, width)]
        return remote(
            part.at[rows, :], target, sends.at[i, step], receives.at[i, step], peer, "task"
        )

    def finish(i, rows, carry):
        valid = valid_rows(small[i], height, breadth)
        _, _, scaled = norm_with(dec_pre[rows, :], totals, scale)
        low = (silu(scaled) * valid).astype(BF)
        part[rows, :] = low
        features[rows, columns_of(task, width)] = low
        for step in range(1, tasks):
            feature_copy(i, rows, step).start()
        return carry

    each_image(geometry, finish, 0)

    def settle(i, rows, carry):
        for step in range(1, tasks):
            feature_copy(i, rows, step, True).wait_recv()
            feature_copy(i, rows, step).wait_send()
            pool_copy(i, step).wait_send()
        return carry

    each_image(geometry, settle, 0)
    for copy in saves:
        copy.wait()


def trunk_forward(geometry, tasks, batches, small, x, enc_taps, dec_taps, scales, choose):
    number, height, breadth = geometry
    pixels = height * breadth
    channels = x.shape[1]
    width = channels // tasks
    windows = window_count(height, breadth)
    tall = shape((x.shape[0], width), F32)
    outs = [
        shape((8, width), F32), shape((8, width), F32), shape(x.shape, BF),
        shape(x.shape, BF), shape(enc_taps.shape, BF), shape(dec_taps.shape, BF),
        tall, tall, shape(x.shape, BF),
    ]
    return exchange_kernel(
        functools.partial(trunk_forward_body, geometry, tasks, batches),
        outs,
        "svvvvv",
        (small, x, enc_taps, dec_taps, scales, choose),
        [
            pltpu.VMEM(tall.shape, F32),
            pltpu.VMEM(tall.shape, F32),
            pltpu.VMEM(x.shape, BF),
            pltpu.VMEM((pixels, 9 * width), F32),
            pltpu.VMEM((number * windows, width), BF),
            pltpu.VMEM((number * windows, channels), BF),
            pltpu.VMEM((x.shape[0], width), BF),
        ]
        + [pltpu.SemaphoreType.DMA((number, tasks))] * 4
        + total_scratch(2, batches)
        + [pltpu.SemaphoreType.DMA((6,))],
        1,
        60,
        flops=4 * x.size * enc_taps.shape[1],
        places_out="vvvhhhhhh",
    )


def head_body(
    geometry, tasks, batches,
    small, features, rows_in, cotangent, scales, counts,
    task_out, grads, upstream, norm_sums,
    pre_one, pre_two, pre_three, hidden, gated, nine, work, lower, out, arrived, sends, receives,
    mine, slots, total_sends, total_receives,
):
    number, height, breadth = geometry
    channels = features.shape[1]
    width = channels // tasks
    windows = task_out.shape[1]
    task = lax.axis_index("task")
    half = work.shape[2]
    _, col = places(height, breadth)
    widen = pool_choice(height, breadth, windows, False).astype(BF)
    narrow = pool_choice(height, breadth, windows, True).astype(BF)
    count = jnp.broadcast_to(counts[2:3, 0:1], (1, channels))
    first = rows_in.at[pl.ds(0, channels), :]
    second = rows_in.at[pl.ds(channels, channels), :]

    def kernel_rows(p):
        return pl.ds((2 + p) * channels, channels)

    def total(k, rows):
        return total_rows(
            k, "batch", batches, list(rows), mine, slots, total_sends, total_receives
        )

    def put_stats(pre, rows, value, valid, carry):
        pre[rows, :] = value
        kept = value * valid
        return carry[0] + col_sum(kept), carry[1] + col_sum(kept * value)

    nothing = zero_rows(2, channels)
    scale_one, scale_two, scale_three = (rows_of(scales, 2 * k, 2) for k in range(3))

    def first_step(i, rows, carry):
        valid = valid_rows(small[i], height, breadth)
        return put_stats(pre_one, rows, dot(features[rows, :], first[...]), valid, carry)

    sums = each_image(geometry, first_step, nothing)
    greet((("task", tasks), ("batch", batches)))
    totals_one = total(0, sums) + [count]

    def second_step(i, rows, carry):
        valid = valid_rows(small[i], height, breadth)
        _, _, scaled = norm_with(pre_one[rows, :], totals_one, scale_one)
        low = (silu(scaled) * valid).astype(BF)
        hidden[rows, :] = low
        return put_stats(pre_two, rows, dot(low, second[...]), valid, carry)

    sums = each_image(geometry, second_step, nothing)
    totals_two = total(1, sums) + [count]

    def third_step(i, rows, carry):
        valid = valid_rows(small[i], height, breadth)
        _, _, scaled = norm_with(pre_two[rows, :], totals_two, scale_two)
        low = (jax.nn.sigmoid(scaled) * features[rows, :].astype(F32)).astype(BF)
        gated[rows, :] = low
        parts = []
        for j in range(channels // half):
            cut = slice(j * half, (j + 1) * half)
            for p in range(9):
                work[p] = dot(low, rows_in[kernel_rows(p), cut])
            parts.append(gather_taps(lambda p: work[p], breadth, col))
        return put_stats(pre_three, rows, jnp.concatenate(parts, axis=1), valid, carry)

    sums = each_image(geometry, third_step, nothing)
    totals_three = total(2, sums) + [count]

    def out_step(i, rows, carry):
        valid = valid_rows(small[i], height, breadth)
        normal, _, scaled = norm_with(pre_three[rows, :], totals_three, scale_three)
        high, low = split(silu(scaled) * valid)
        mean = (dot(narrow, high) + dot(narrow, low)) * 0.25
        task_out[i] = mean.astype(BF)
        dy = silu_back(scaled) * dot(widen, cotangent[i]) * 0.25 * valid
        lower[rows, :] = dy
        return carry[0] + col_sum(dy), carry[1] + col_sum(dy * normal)

    sums = each_image(geometry, out_step, nothing)
    sums_three = total(3, sums)

    def third_back(i, rows, carry):
        valid = valid_rows(small[i], height, breadth)
        normal, inverse, _ = norm_with(pre_three[rows, :], totals_three, scale_three)
        dz = norm_back_with(lower[rows, :], normal, inverse, count, sums_three, scale_three, valid)
        for p, moved in enumerate(spread_taps(dz, breadth, col)):
            nine[p, rows, :] = moved.astype(BF)
        flow = None
        for p in range(9):
            piece = dot_nt(nine[p, rows, :], rows_in[kernel_rows(p), :])
            flow = piece if flow is None else flow + piece
        lower[rows, :] = flow
        normal, _, scaled = norm_with(pre_two[rows, :], totals_two, scale_two)
        gate = jax.nn.sigmoid(scaled)
        dy = flow * features[rows, :].astype(F32) * gate * (1.0 - gate) * valid
        pre_three[rows, :] = dy
        return carry[0] + col_sum(dy), carry[1] + col_sum(dy * normal)

    sums = each_image(geometry, third_back, nothing)
    sums_two = total(4, sums)

    def second_back(i, rows, carry):
        valid = valid_rows(small[i], height, breadth)
        normal, inverse, scaled = norm_with(pre_two[rows, :], totals_two, scale_two)
        dz = norm_back_with(
            pre_three[rows, :], normal, inverse, count, sums_two, scale_two, valid
        ).astype(BF)
        out[rows, :] = dz
        lower[rows, :] = lower[rows, :] * jax.nn.sigmoid(scaled)
        normal, _, scaled = norm_with(pre_one[rows, :], totals_one, scale_one)
        dy = silu_back(scaled) * dot_nt(dz, second[...]) * valid
        pre_three[rows, :] = dy
        return carry[0] + col_sum(dy), carry[1] + col_sum(dy * normal)

    sums = each_image(geometry, second_back, nothing)
    sums_one = total(5, sums)
    grads[pl.ds(channels, channels), :] = dot_tn(hidden[...], out[...]).astype(grads.dtype)

    def flow_copy(i, rows, step, incoming=False):
        peer = lax.rem(task + (tasks - step if incoming else step), tasks)
        return remote(
            out.at[rows, columns_of(peer, width)], arrived.at[step - 1, rows, :],
            sends.at[i, step], receives.at[i, step], peer, "task",
        )

    def first_back(i, rows, carry):
        valid = valid_rows(small[i], height, breadth)
        normal, inverse, _ = norm_with(pre_one[rows, :], totals_one, scale_one)
        dz = norm_back_with(
            pre_three[rows, :], normal, inverse, count, sums_one, scale_one, valid
        ).astype(BF)
        hidden[rows, :] = dz
        flow = (lower[rows, :] + dot_nt(dz, first[...])) * valid
        out[rows, :] = flow.astype(BF)
        for step in range(1, tasks):
            flow_copy(i, rows, step).start()
        return carry

    each_image(geometry, first_back, 0)
    grads[pl.ds(0, channels), :] = dot_tn(features[...], hidden[...]).astype(grads.dtype)

    def tap(p, carry):
        rows = pl.ds(pl.multiple_of((2 + p) * channels, channels), channels)
        grads[rows, :] = dot_tn(gated[...], nine[p]).astype(grads.dtype)
        return carry

    lax.fori_loop(0, 9, tap, 0)
    put_sums(norm_sums, sums_one + sums_two + sums_three)

    def settle(i, rows, carry):
        for step in range(1, tasks):
            flow_copy(i, rows, step, True).wait_recv()
        flow = out[rows, columns_of(task, width)].astype(F32)
        for step in range(1, tasks):
            flow = flow + arrived[step - 1, rows, :].astype(F32)
        upstream[rows, :] = flow
        for step in range(1, tasks):
            flow_copy(i, rows, step).wait_send()
        return carry

    each_image(geometry, settle, 0)


def head(geometry, tasks, batches, small, features, rows_in, cotangent, scales, counts):
    number, height, breadth = geometry
    pixels = height * breadth
    total, channels = features.shape
    width = channels // tasks
    return exchange_kernel(
        functools.partial(head_body, geometry, tasks, batches),
        [
            shape((number, pixels // 4, channels), BF),
            shape(rows_in.shape, BF),
            shape((total, width), F32),
            shape((8, channels), F32),
        ],
        "svvvvv",
        (small, features, rows_in, cotangent, scales, counts),
        [
            pltpu.VMEM(features.shape, F32),
            pltpu.VMEM(features.shape, F32),
            pltpu.VMEM(features.shape, F32),
            pltpu.VMEM(features.shape, BF),
            pltpu.VMEM(features.shape, BF),
            pltpu.VMEM((9,) + features.shape, BF),
            pltpu.VMEM((9, pixels, min(channels, 256)), F32),
            pltpu.VMEM(features.shape, F32),
            pltpu.VMEM(features.shape, BF),
            pltpu.VMEM((tasks - 1, total, width), BF),
        ]
        + [pltpu.SemaphoreType.DMA((number, tasks))] * 2
        + total_scratch(6, batches),
        2,
        60,
        flops=6 * total * channels * rows_in.shape[0],
    )


def trunk_backward_body(
    geometry, tasks, batches, summing,
    small, upstream, enc_totals, dec_totals, scales, choose_row, *rest,
):
    kept, rest = rest[:6], rest[6:]
    if summing:
        head_grads, rest = rest[0], rest[1:]
    (enc_grad, dec_grad, flow_out, norm_sums), rest = rest[:4], rest[4:]
    if summing:
        head_owned, rest = rest[0], rest[1:]
    (x, enc_taps, dec_taps, enc_pre, dec_pre, spread), rest = rest[:6], rest[6:]
    (
        nine, change, packed, arrived, pooled, sends, receives,
        mine, slots, total_sends, total_receives, loaded,
    ) = rest[:12]
    head_stages = [lambda: None] * 3
    if summing:
        near, paired, far, near_send, near_receive, far_send, far_receive, own, own_loaded = rest[12:]
        place, core, chips = pair_place(batches)
        count = near.shape[1]

        def own_load(step):
            chip = lax.rem(place + step, chips)
            source = block_rows(head_grads, 2 * chip + core, count)
            return pltpu.make_async_copy(source, own.at[step], own_loaded.at[step])

        for step in range(chips):
            own_load(step).start()
        *head_stages, head_end = pair_sum(
            batches, lambda index: block_rows(head_grads, index, count),
            lambda step: own[step].astype(F32), near, paired, far,
            (near_send, near_receive, far_send, far_receive),
        )
    head_start, head_middle, head_relay = head_stages
    targets = (x, enc_taps, dec_taps, enc_pre, dec_pre, spread)
    loads = [pltpu.make_async_copy(a, b, loaded.at[k]) for k, (a, b) in enumerate(zip(kept, targets))]
    for k in (4, 2, 5, 3, 1, 0):
        loads[k].start()
    number, height, breadth = geometry
    channels = x.shape[1]
    width = enc_pre.shape[1]
    windows = window_count(height, breadth)
    task = lax.axis_index("task")
    _, col = places(height, breadth)
    widen = pool_choice(height, breadth, windows, False).astype(BF)
    narrow = pool_choice(height, breadth, windows, True)
    nothing = zero_rows(2, width)

    def total(k, rows):
        return total_rows(
            k, "batch", batches, list(rows), mine, slots, total_sends, total_receives
        )

    def change_of(pre, totals, scale, flow):
        def image(i, rows, carry):
            valid = valid_rows(small[i], height, breadth)
            normal, _, scaled = norm_with(pre[rows, :], totals, scale)
            dy = silu_back(scaled) * flow(i, rows) * valid
            change[rows, :] = dy
            return carry[0] + col_sum(dy), carry[1] + col_sum(dy * normal)

        return each_image(geometry, image, nothing)

    def back(pre, totals, scale, sums, taps, put):
        def image(i, rows, carry):
            valid = valid_rows(small[i], height, breadth)
            normal, inverse, _ = norm_with(pre[rows, :], totals, scale)
            dz = norm_back_with(change[rows, :], normal, inverse, totals[2], sums, scale, valid)
            for p, moved in enumerate(spread_taps(dz, breadth, col)):
                nine[rows, p * width : (p + 1) * width] = moved.astype(BF)
            put(i, rows, dot_nt(nine[rows, :], taps[...]) * valid)
            return carry

        each_image(geometry, image, 0)

    totals = rows_of(dec_totals, 0, 3)
    scale = rows_of(scales, 2, 2)
    loads[4].wait()
    sums = change_of(dec_pre, totals, scale, lambda i, rows: upstream[rows, :])
    greet((("task", tasks), ("batch", batches)))
    head_start()
    dec_sums = total(0, sums)
    if summing:
        for step in range(chips):
            own_load(step).wait()

    def copy_of(i, step, incoming=False):
        rows = window_rows(i, windows)
        peer = lax.rem(task + (tasks - step if incoming else step), tasks)
        return remote(
            packed.at[rows, columns_of(peer, width)], arrived.at[step - 1, rows, :],
            sends.at[i, step], receives.at[i, step], peer, "task",
        )

    def put_packed(i, rows, flow):
        chosen = (narrow * choose_row[i]).astype(BF)
        packed[window_rows(i, windows), :] = dot(chosen, flow.astype(BF)).astype(BF)
        for step in range(1, tasks):
            copy_of(i, step).start()

    loads[2].wait()
    back(dec_pre, totals, scale, dec_sums, dec_taps, put_packed)
    loads[5].wait()
    head_middle()
    dec_grad[...] = dot_tn(spread[...], nine[...])

    def collect(i, carry):
        for step in range(1, tasks):
            copy_of(i, step, True).wait_recv()
        rows = window_rows(i, windows)
        flow = packed[rows, columns_of(task, width)].astype(F32)
        for step in range(1, tasks):
            flow = flow + arrived[step - 1, rows, :].astype(F32)
        pooled[rows, :] = flow
        for step in range(1, tasks):
            copy_of(i, step).wait_send()
        return carry

    lax.fori_loop(0, number, collect, 0)

    def widened(i, rows):
        high, low = split(pooled[window_rows(i, windows), :])
        return (dot(widen, high) + dot(widen, low)) * 0.25

    totals = rows_of(enc_totals, 0, 3)
    scale = rows_of(scales, 0, 2)
    loads[3].wait()
    sums = change_of(enc_pre, totals, scale, widened)
    enc_sums = total(1, sums)
    head_relay()

    def put_flow(i, rows, flow):
        flow_out[rows, :] = flow.astype(BF)

    loads[1].wait()
    back(enc_pre, totals, scale, enc_sums, enc_taps, put_flow)
    loads[0].wait()
    enc_grad[...] = dot_tn(x[...], nine[...])
    put_sums(norm_sums, enc_sums + dec_sums)
    if summing:
        head_owned[...] = head_end().astype(BF)


def trunk_backward(
    geometry, tasks, batches, small, upstream, enc_totals, dec_totals, scales, choose_row,
    head_grads, kept,
):
    number, height, breadth = geometry
    x, enc_taps, dec_taps = kept[:3]
    total, channels = x.shape
    width = channels // tasks
    windows = window_count(height, breadth)
    head_rows = head_grads.shape[0]
    summing = head_rows % (16 * batches) == 0
    outs = [
        shape(enc_taps.shape, F32),
        shape(dec_taps.shape, F32),
        shape(x.shape, BF),
        shape((8, width), F32),
    ]
    specs = "svvvvvhhhhhh"
    args = (small, upstream, enc_totals, dec_totals, scales, choose_row, *kept)
    scratch = []
    if summing:
        outs.append(shape((head_rows // batches, channels), BF))
        specs += "h"
        args += (head_grads,)
        scratch = pair_scratch(batches, head_rows, channels, BF) + [
            pltpu.VMEM((batches // 2, head_rows // batches, channels), BF),
            pltpu.SemaphoreType.DMA((batches // 2,)),
        ]
    made = exchange_kernel(
        functools.partial(trunk_backward_body, geometry, tasks, batches, summing),
        outs,
        specs,
        args,
        [pltpu.VMEM(a.shape, a.dtype) for a in kept]
        + [
            pltpu.VMEM((total, 9 * width), BF),
            pltpu.VMEM((total, width), F32),
            pltpu.VMEM((number * windows, channels), BF),
            pltpu.VMEM((tasks - 1, number * windows, width), BF),
            pltpu.VMEM((number * windows, width), F32),
        ]
        + [pltpu.SemaphoreType.DMA((number, tasks))] * 2
        + total_scratch(2, batches)
        + [pltpu.SemaphoreType.DMA((6,))]
        + scratch,
        3,
        60,
        flops=8 * x.size * enc_taps.shape[1],
    )
    if summing:
        return made
    return *made, lax.psum_scatter(head_grads, "batch", scatter_dimension=0, tiled=True)


def exchange(body, outs, args, scratch, identity, vmem=60):
    size = sum(o.size * o.dtype.itemsize for o in outs) + sum(a.size * a.dtype.itemsize for a in args)
    return pl.pallas_call(
        body,
        out_shape=tuple(outs),
        in_specs=[VMEM_SPEC] * len(args),
        out_specs=tuple(VMEM_SPEC for _ in outs),
        scratch_shapes=list(scratch),
        compiler_params=pltpu.CompilerParams(
            vmem_limit_bytes=vmem * MIB, collective_id=identity, has_side_effects=True
        ),
        cost_estimate=pl.CostEstimate(flops=0, bytes_accessed=size, transcendentals=0),
    )(*args)


def block_of(ref, place, size, dim):
    length = ref.shape[dim] // size
    start = place * length
    if dim == 0:
        return ref.at[pl.ds(pl.multiple_of(start, 8), length), :]
    return ref.at[:, pl.ds(pl.multiple_of(start, 128), length)]


def gather_body(axis, size, dims, *refs):
    count = len(dims)
    sources, targets = refs[:count], refs[count : 2 * count]
    sends, receives, own = refs[2 * count :]
    greet(((axis, size),))
    me = lax.axis_index(axis)
    copies = []
    for k in range(count):
        mine = block_of(targets[k], me, size, dims[k])
        for step in range(1, size):
            peer = lax.rem(me + step, size)
            copy = remote(sources[k], mine, sends.at[k, step], receives.at[k, me], peer, axis)
            copy.start()
            copies.append(copy)
    locals_ = []
    for k in range(count):
        mine = block_of(targets[k], me, size, dims[k])
        copy = pltpu.make_async_copy(sources[k], mine, own.at[k])
        copy.start()
        locals_.append(copy)
    for copy in locals_:
        copy.wait()
    for k in range(count):
        for step in range(1, size):
            peer = lax.rem(me + size - step, size)
            theirs = block_of(targets[k], peer, size, dims[k])
            remote(
                sources[k], theirs, sends.at[k, step], receives.at[k, peer], peer, axis
            ).wait_recv()
    for copy in copies:
        copy.wait_send()


def gather_over(axis, size, arrays, dims, identity):
    outs = []
    for x, dim in zip(arrays, dims):
        full = list(x.shape)
        full[dim] *= size
        outs.append(shape(full, x.dtype))
    count = len(arrays)
    return exchange(
        functools.partial(gather_body, axis, size, tuple(dims)),
        outs,
        arrays,
        [
            pltpu.SemaphoreType.DMA((count, size)),
            pltpu.SemaphoreType.DMA((count, size)),
            pltpu.SemaphoreType.DMA((count,)),
        ],
        identity,
    )


def to_taps_body(index, slots, enc, dec, wide, tap):
    count = slots.shape[0]
    channels = enc.shape[0]
    width = slots.shape[1]
    step = 1024

    def widen(i, carry):
        rows = pl.ds(pl.multiple_of(i * step, step), step)
        wide[rows, :] = slots[rows, :].astype(F32)
        return carry

    lax.fori_loop(0, count // step, widen, 0)
    group = 32
    for p in range(18):

        def fetch(i, carry):
            base = i * group
            for u in range(group):
                tap[pl.ds(base + u, 1), :] = wide[pl.ds(index[p * channels + base + u], 1), :]
            return carry

        lax.fori_loop(0, channels // group, fetch, 0)
        out = enc if p < 9 else dec
        q = p % 9
        out[:, q * width : (q + 1) * width] = tap[...].astype(BF)


def to_taps(index, slots, channels):
    width = slots.shape[1]
    return run(
        to_taps_body,
        [shape((channels, 9 * width), BF)] * 2,
        "sv",
        (index, slots),
        [pltpu.VMEM(slots.shape, F32), pltpu.VMEM((channels, width), F32)],
        vmem=60,
        flops=10000 * MIB,
    )


def to_slots_body(index, enc, dec, slots, wide):
    count = slots.shape[0]
    channels = enc.shape[0]
    width = slots.shape[1]
    step = 1024
    group = 32
    for p in range(18):
        source = enc if p < 9 else dec
        q = p % 9

        def place(i, carry):
            base = pl.multiple_of(i * group, group)
            values = source[pl.ds(base, group), q * width : (q + 1) * width]
            for u in range(group):
                wide[pl.ds(index[p * channels + base + u], 1), :] = values[u : u + 1, :]
            return carry

        lax.fori_loop(0, channels // group, place, 0)

    def narrow(i, carry):
        rows = pl.ds(pl.multiple_of(i * step, step), step)
        slots[rows, :] = wide[rows, :].astype(BF)
        return carry

    lax.fori_loop(0, count // step, narrow, 0)


def to_slots(index, enc, dec):
    width = enc.shape[1] // 9
    dims = (index.shape[0], width)
    return run(
        to_slots_body, [shape(dims, BF)], "svv", (index, enc, dec), [pltpu.VMEM(dims, F32)], vmem=60
    )[0]


def adam(gradient, moment_one, moment_two):
    new_one = BETA_ONE * moment_one + (1.0 - BETA_ONE) * gradient
    new_two = BETA_TWO * moment_two + (1.0 - BETA_TWO) * gradient * gradient
    direction = (
        new_one / (1.0 - BETA_ONE**STEP) / (jnp.sqrt(new_two / (1.0 - BETA_TWO**STEP)) + ADAM_EPS)
    )
    return new_one, new_two, direction


def pair_place(batches):
    me = lax.axis_index("batch")
    place = lax.div(me, 2)
    return place, me - 2 * place, batches // 2


def greet_pairs(tasks, batches):
    place, core, chips = pair_place(batches)
    task = lax.axis_index("task")
    barrier = pltpu.get_barrier_semaphore()

    def signal(device):
        pl.semaphore_signal(barrier, inc=1, device_id=device, device_id_type=MESH)

    for step in range(1, tasks):
        signal({"task": lax.rem(task + step, tasks)})
    signal({"batch": 2 * place + 1 - core})
    for step in range(1, chips):
        signal({"batch": 2 * lax.rem(place + step, chips) + core})
    pl.semaphore_wait(barrier, tasks - 1 + chips)


def block_rows(ref, index, count):
    return ref.at[pl.ds(pl.multiple_of(index * count, 8), count), :]


def far_first(chips):
    return sorted(range(chips), key=lambda step: -min(step, chips - step))


def pair_sum(batches, rows_of_block, own_block, near, paired, far, sems):
    place, core, chips = pair_place(batches)
    count = near.shape[1]
    near_send, near_receive, far_send, far_receive = sems
    other = 2 * place + 1 - core
    ring = chips == 4 and count % 32 == 0
    half = count // 2
    halves = (pl.ds(0, half), pl.ds(half, half))

    def near_copy(step):
        chip = lax.rem(place + step, chips)
        return remote(rows_of_block(2 * chip + 1 - core), near.at[step],
                      near_send.at[step], near_receive.at[step], other, "batch")

    def far_copy(step, incoming=False):
        chip = lax.rem(place + (chips - step if incoming else step), chips)
        return remote(paired.at[step], far.at[step], far_send.at[step], far_receive.at[step],
                      2 * chip + core, "batch")

    def ring_copy(which, way):
        chip = lax.rem(place + (1 if way == 0 else chips - 1), chips)
        if which == 0:
            source, target = paired.at[2, halves[way], :], far.at[2 + way, halves[0], :]
        else:
            cut = halves[way] if which == 2 else halves[1 - way]
            source, target = paired.at[1 if way == 0 else 3, cut, :], far.at[way, cut, :]
        k = 2 * which + way
        return remote(source, target, far_send.at[k], far_receive.at[k], 2 * chip + core, "batch")

    def start():
        for step in far_first(chips):
            near_copy(step).start()

    def middle():
        for step in far_first(chips):
            near_copy(step).wait_recv()
            if step:
                paired[step] = (own_block(step) + near[step].astype(F32)).astype(paired.dtype)
                if not ring:
                    far_copy(step).start()
                elif step == 2:
                    ring_copy(0, 0).start()
                    ring_copy(0, 1).start()
                else:
                    ring_copy(1, 0 if step == 1 else 1).start()

    def relay():
        if not ring:
            return
        for way in range(2):
            ring_copy(0, way).wait_recv()
            step = 1 if way == 0 else 3
            total = paired[step, halves[way], :].astype(F32) + far[2 + way, halves[0], :].astype(F32)
            paired[step, halves[way], :] = total.astype(paired.dtype)
            ring_copy(2, way).start()

    def end():
        total = own_block(0) + near[0].astype(F32)
        if ring:
            for way in range(2):
                ring_copy(1, way).wait_recv()
                ring_copy(2, way).wait_recv()
                total = total + far[way].astype(F32)
            for k in range(3):
                for way in range(2):
                    ring_copy(k, way).wait_send()
        else:
            for step in range(1, chips):
                far_copy(step, True).wait_recv()
                total = total + far[step].astype(F32)
            for step in range(1, chips):
                far_copy(step).wait_send()
        for step in range(chips):
            near_copy(step).wait_send()
        return total

    return start, middle, relay, end


def blocks_in(source, batches, count):
    place, core, chips = pair_place(batches)

    def own(step):
        chip = lax.rem(place + step, chips)
        return block_rows(source, 2 * chip + core, count)[...].astype(F32)

    return (lambda index: block_rows(source, index, count)), own


def pair_scratch(batches, rows, width, kind):
    chips = batches // 2
    return [pltpu.VMEM((chips, rows // batches, width), kind)] * 3 + [
        pltpu.SemaphoreType.DMA((max(chips, 6),))
    ] * 4


def chip_spread(batches, block, sends, receives):
    place, core, chips = pair_place(batches)
    count = block(place).shape[0]
    ring = chips == 4 and count % 32 == 0
    half = count // 2

    def copy(step, incoming=False):
        peer = lax.rem(place + (chips - step if incoming else step), chips)
        ref = block(peer if incoming else place)
        return remote(ref, ref, sends.at[step], receives.at[step], 2 * peer + core, "batch")

    def pass_on(way, incoming=False):
        step = 1 if way == 0 else chips - 1
        peer = lax.rem(place + (chips - step if incoming else step), chips)
        home = lax.rem(place + (2 if incoming else chips - step), chips)
        ref = block(home).at[pl.ds(way * half, half), :]
        k = 2 if way == 0 else 0
        return remote(ref, ref, sends.at[k], receives.at[k], 2 * peer + core, "batch")

    steps = (1, chips - 1) if ring else tuple(range(1, chips))

    def start():
        for step in steps:
            copy(step).start()

    def relay():
        if ring:
            for way, step in enumerate(steps):
                copy(step, True).wait_recv()
                pass_on(way).start()

    def settle():
        if ring:
            for way in range(2):
                pass_on(way, True).wait_recv()
        else:
            for step in steps:
                copy(step, True).wait_recv()

    def drain():
        for step in steps:
            copy(step).wait_send()
        if ring:
            for way in range(2):
                pass_on(way).wait_send()

    return start, relay, settle, drain


def collect_body(
    tasks, batches,
    slots, flow, sums,
    input_grad, owned, part, norm_sums,
    near, paired, far, near_send, near_receive, far_send, far_receive,
    flow_in, flow_send, flow_receive, send, receive, sum_send, sum_receive,
):
    task = lax.axis_index("task")
    width = part.shape[1]
    pixels = input_grad.shape[0]

    def peer_of(step, incoming):
        return lax.rem(task + (tasks - step if incoming else step), tasks)

    def flow_copy(step, incoming=False):
        peer = peer_of(step, incoming)
        return remote(block_rows(flow, peer, pixels), flow_in.at[step - 1], flow_send.at[step],
                      flow_receive.at[step], peer, "task")

    def sum_copy(step, incoming=False):
        peer = peer_of(step, incoming)
        home = peer if incoming else task
        return remote(sums, norm_sums.at[:, columns_of(home, width)], sum_send.at[step],
                      sum_receive.at[step], peer, "task")

    def part_copy(step, incoming=False):
        peer = peer_of(step, incoming)
        home = peer if incoming else task
        return remote(part, owned.at[:, columns_of(home, width)], send.at[step], receive.at[step],
                      peer, "task")

    greet_pairs(tasks, batches)
    start, middle, relay, end = pair_sum(
        batches, *blocks_in(slots, batches, near.shape[1]), near, paired, far,
        (near_send, near_receive, far_send, far_receive),
    )
    start()
    for step in range(1, tasks):
        sum_copy(step).start()
        flow_copy(step).start()
    norm_sums[:, columns_of(task, width)] = sums[...]
    middle()
    relay()
    total = end().astype(BF)
    part[...] = total
    for step in range(1, tasks):
        part_copy(step).start()
    owned[:, columns_of(task, width)] = total
    total = block_rows(flow, task, pixels)[...].astype(F32)
    for step in range(1, tasks):
        flow_copy(step, True).wait_recv()
        total = total + flow_in[step - 1].astype(F32)
    input_grad[...] = total
    for step in range(1, tasks):
        sum_copy(step, True).wait_recv()
        part_copy(step, True).wait_recv()
        sum_copy(step).wait_send()
        part_copy(step).wait_send()
        flow_copy(step).wait_send()


def collect(tasks, batches, slots, flow, sums):
    count, width = slots.shape
    rows = count // batches
    pixels, channels = flow.shape[0] // tasks, flow.shape[1]
    return exchange_kernel(
        functools.partial(collect_body, tasks, batches),
        [
            shape((pixels, channels), F32),
            shape((rows, channels), BF),
            shape((rows, width), BF),
            shape((8, channels), F32),
        ],
        "vvv",
        (slots, flow, sums),
        pair_scratch(batches, count, width, BF)
        + [pltpu.VMEM((tasks - 1, pixels, channels), BF)]
        + [pltpu.SemaphoreType.DMA((tasks,))] * 6,
        5,
        60,
        flops=20000 * MIB,
    )


def soap_rows(cuts, grad, owners, state, low, first):
    count = owners.shape[1]
    total = grad.shape[0]

    def chunk(i, carry):
        rows = pl.ds(pl.multiple_of(i * (total // cuts), 8), total // cuts)
        values = grad[rows, :].astype(F32)
        rotated = None
        for m in range(count):
            part = dot((values * owners[rows, m : m + 1]).astype(BF), low[first + m])
            rotated = part if rotated is None else rotated + part
        new_one, new_two, direction = adam(rotated, state[1, rows, :], state[2, rows, :])
        state[1, rows, :] = new_one
        state[2, rows, :] = new_two
        stepped = None
        for m in range(count):
            part = dot_nt((direction * owners[rows, m : m + 1]).astype(BF), low[first + m])
            stepped = part if stepped is None else stepped + part
        old = state[0, rows, :]
        state[0, rows, :] = old - LEARN_MATRIX * (stepped + DECAY_MATRIX * old)
        return carry

    lax.fori_loop(0, cuts, chunk, 0)


def factor_rows(values, identity, turn):
    size, width = values.shape
    sub = lax.broadcasted_iota(jnp.int32, (size, width), 0)
    rolled = pltpu.roll(values, turn, 1)
    columns = [jnp.broadcast_to(rolled[:, j : j + 1], (size, width)) for j in range(size)]
    scale = jnp.zeros((size, width), F32)
    for j in range(size):
        root = lax.rsqrt(columns[j][j : j + 1, :])
        scale = jnp.where(sub == j, root, scale)
        lower = jnp.where(sub > j, columns[j] * root, 0.0)
        values = values - lower * (values[j : j + 1, :] * root)
        identity = identity - lower * (identity[j : j + 1, :] * root)
        for i in range(j + 1, size):
            columns[i] = columns[i] - lower * (columns[i][j : j + 1, :] * root)
    return values * scale, identity * scale


GROUP = 16
PANEL = 128


def renew_panel(k, product, made, tables, inverses):
    count, size = product.shape[0], product.shape[1]
    here = slice(k * PANEL, (k + 1) * PANEL)
    row = lax.broadcasted_iota(jnp.int32, (PANEL, PANEL), 0)
    col = lax.broadcasted_iota(jnp.int32, (PANEL, PANEL), 1)
    unit = jnp.where(row == col, 1.0, 0.0).astype(F32)
    for n in range(count):
        tables[n][:, :PANEL] = dot3(dot_tn, product[n, :, here], product[n, :, here])
        tables[n][:, PANEL:] = unit

    def group(q, carry):
        rows = pl.ds(pl.multiple_of(q * GROUP, GROUP), GROUP)
        turn = lax.rem(PANEL - q * GROUP, PANEL)
        done = [
            factor_rows(tables[n][rows, :PANEL], tables[n][rows, PANEL:], turn)
            for n in range(count)
        ]
        for n in range(count):
            upper, inverse = done[n]
            inverses[n][rows, :] = inverse
            both = jnp.concatenate([upper, inverse], axis=1)
            tables[n][...] = tables[n][...] - dot3(dot_tn, upper, both)
        return carry

    lax.fori_loop(0, PANEL // GROUP, group, 0)
    for n in range(count):
        turned = dot3(dot_nt, product[n, :, here], inverses[n][...])
        made[n, :, here] = turned
        if k < size // PANEL - 1:
            rest = slice((k + 1) * PANEL, size)
            product[n, :, rest] = product[n, :, rest] - dot3(
                dot, turned, dot3(dot_tn, turned, product[n, :, rest])
            )


def rows_body(
    tasks, batches, cuts,
    grad, part, owners, head_grad, head_owners,
    weight, one, two, head_weight, head_one, head_two, basis, head_basis,
    state_new, head_state_new, grams, head_grams,
    state, head_state, mine, head_mine, bases, low,
    near, paired, far, near_send, near_receive, far_send, far_receive,
    head_near, head_paired, head_far, *rest,
):
    head_sems = rest[:4]
    chip_send, chip_receive, task_send, task_receive, pair_send, pair_receive, load, save = rest[4:]
    task = lax.axis_index("task")
    place, core, chips = pair_place(batches)
    width = part.shape[1]
    channels = grad.shape[1]
    count, head_count = near.shape[1], head_near.shape[1]
    trunk_total, head_total = owners.shape[1], head_owners.shape[1]

    moves = [
        (basis, bases.at[pl.ds(0, trunk_total)]),
        (head_basis, bases.at[pl.ds(trunk_total, head_total)]),
        (weight, state.at[0]),
        (one, state.at[1]),
        (two, state.at[2]),
        (head_weight, head_state.at[0]),
        (head_one, head_state.at[1]),
        (head_two, head_state.at[2]),
    ]
    loads = [pltpu.make_async_copy(a, b, load.at[k]) for k, (a, b) in enumerate(moves)]
    for copy in loads:
        copy.start()
    for m in range(head_total):
        held = (head_grad[...].astype(F32) * head_owners[:, m : m + 1]).astype(BF)
        head_mine[m * channels : (m + 1) * channels, :] = dot_tn(held, head_grad[...]).astype(
            head_mine.dtype
        )
    greet_pairs(tasks, batches)
    head_start, head_middle, head_relay, head_end = pair_sum(
        batches, *blocks_in(head_mine, batches, head_count), head_near, head_paired, head_far,
        head_sems,
    )
    head_start()
    for m in range(trunk_total):
        held = (grad[...].astype(F32) * owners[:, m : m + 1]).astype(BF)
        mine[m * channels : (m + 1) * channels, :] = dot_tn(held, part[...]).astype(mine.dtype)
    start, middle, relay, end = pair_sum(
        batches, *blocks_in(mine, batches, count), near, paired, far,
        (near_send, near_receive, far_send, far_receive),
    )
    start()
    head_middle()
    middle()
    head_relay()
    relay()

    def trunk_block(chip, home, which):
        rows = pl.ds(pl.multiple_of((2 * chip + which) * count, 8), count)
        return grams.at[rows, columns_of(home, width)]

    def head_block(chip, which):
        return block_rows(head_grams, 2 * chip + which, head_count)

    trunk_spread = chip_spread(
        batches, lambda chip: trunk_block(chip, task, core), chip_send.at[0], chip_receive.at[0]
    )
    head_spread = chip_spread(
        batches, lambda chip: head_block(chip, core), chip_send.at[1], chip_receive.at[1]
    )

    def task_copy(step, hop, incoming=False):
        peer = lax.rem(task + (tasks - step if incoming else step), tasks)
        chip = lax.rem(place + chips - hop, chips)
        block = trunk_block(chip, peer if incoming else task, core)
        return remote(block, block, task_send.at[step, hop], task_receive.at[step, hop], peer, "task")

    def pair_copy(kind, hop, incoming=False):
        chip = lax.rem(place + chips - hop, chips)
        which = 1 - core if incoming else core
        home = lax.rem(task + tasks - kind, tasks)
        block = head_block(chip, which) if kind == tasks else trunk_block(chip, home, which)
        return remote(block, block, pair_send.at[kind, hop], pair_receive.at[kind, hop],
                      2 * place + 1 - core, "batch")

    for copy in loads[:5]:
        copy.wait()
    for m in range(trunk_total + head_total):
        low[m] = bases[m].astype(BF)
    total = end().astype(grams.dtype)
    trunk_block(place, task, core)[...] = total
    trunk_spread[0]()
    for step in range(1, tasks):
        task_copy(step, 0).start()
    pair_copy(0, 0).start()
    soap_rows(cuts, grad, owners, state, low, 0)
    saves = [
        pltpu.make_async_copy(state, state_new, save.at[0]),
        pltpu.make_async_copy(head_state, head_state_new, save.at[1]),
    ]
    saves[0].start()
    total = head_end().astype(head_grams.dtype)
    head_block(place, core)[...] = total
    head_spread[0]()
    pair_copy(tasks, 0).start()
    trunk_spread[1]()
    trunk_spread[2]()
    for hop in range(1, chips):
        for step in range(1, tasks):
            task_copy(step, hop).start()
        pair_copy(0, hop).start()
    head_spread[1]()
    for copy in loads[5:]:
        copy.wait()
    soap_rows(cuts, head_grad, head_owners, head_state, low, trunk_total)
    saves[1].start()
    for hop in range(chips):
        for step in range(1, tasks):
            task_copy(step, hop, True).wait_recv()
            pair_copy(step, hop).start()
    head_spread[2]()
    for hop in range(1, chips):
        pair_copy(tasks, hop).start()
    for hop in range(chips):
        for kind in range(tasks + 1):
            pair_copy(kind, hop, True).wait_recv()
    for copy in saves:
        copy.wait()
    for hop in range(chips):
        for kind in range(tasks + 1):
            pair_copy(kind, hop).wait_send()
        for step in range(1, tasks):
            task_copy(step, hop).wait_send()
    trunk_spread[3]()
    head_spread[3]()


def renew_body(
    state, head_state, grams, head_grams, stat, head_stat, basis, head_basis,
    weight_new, one_new, two_new, head_weight_new, head_one_new, head_two_new,
    stat_new, head_stat_new, basis_new, head_basis_new,
    stats, product, made, save, *work,
):
    trunk_total, head_total = stat.shape[0], head_stat.shape[0]
    channels = stat.shape[1]
    count = trunk_total + head_total
    tables, inverses = work[:count], work[count:]
    sources = [state.at[k] for k in range(3)] + [head_state.at[k] for k in range(3)]
    targets = [weight_new, one_new, two_new, head_weight_new, head_one_new, head_two_new]
    saves = [pltpu.make_async_copy(a, b, save.at[k]) for k, (a, b) in enumerate(zip(sources, targets))]
    for copy in saves:
        copy.start()
    for m in range(count):
        first = m < trunk_total
        place = m if first else m - trunk_total
        gram = (grams if first else head_grams)[place * channels : (place + 1) * channels, :]
        old = (stat if first else head_stat)[place]
        stats[m] = STAT_DECAY * old + (1.0 - STAT_DECAY) * gram.astype(F32)
        product[m] = dot3(dot, stats[m], (basis if first else head_basis)[place])
    groups = ((0, trunk_total, stat_new, basis_new), (trunk_total, head_total, head_stat_new, head_basis_new))
    for begin, size, out, _ in groups:
        copy = pltpu.make_async_copy(stats.at[pl.ds(begin, size)], out, save.at[len(saves)])
        copy.start()
        saves.append(copy)
    for k in range(channels // PANEL):
        renew_panel(k, product, made, tables, inverses)
        cut = pl.ds(k * PANEL, PANEL)
        for begin, size, _, out in groups:
            copy = pltpu.make_async_copy(
                made.at[pl.ds(begin, size), :, cut], out.at[:, :, cut], save.at[len(saves)]
            )
            copy.start()
            saves.append(copy)
    for copy in saves:
        copy.wait()


def finish(tasks, batches, local_grads, rows, matrices):
    grad, part, owners, head_grad, head_owners = local_grads
    stat, head_stat, basis, head_basis = matrices
    channels, width = grad.shape[1], part.shape[1]
    trunk_total, head_total = owners.shape[1], head_owners.shape[1]
    gram_rows, head_rows = trunk_total * channels, head_total * channels
    chips = batches // 2
    kind = BF if gram_rows % (16 * batches) == 0 else F32
    head_kind = BF if head_rows % (16 * batches) == 0 else F32
    cuts = 4 if grad.shape[0] % 64 == 0 and head_grad.shape[0] % 64 == 0 else 1
    square = (trunk_total + head_total, channels, channels)
    made = exchange_kernel(
        functools.partial(rows_body, tasks, batches, cuts),
        [
            shape((3,) + grad.shape, F32),
            shape((3,) + head_grad.shape, F32),
            shape((gram_rows, channels), kind),
            shape((head_rows, channels), head_kind),
        ],
        "vvvvvhhhhhhhh",
        (*local_grads, *rows, basis, head_basis),
        [
            pltpu.VMEM((3,) + grad.shape, F32),
            pltpu.VMEM((3,) + head_grad.shape, F32),
            pltpu.VMEM((gram_rows, width), kind),
            pltpu.VMEM((head_rows, channels), head_kind),
            pltpu.VMEM(square, F32),
            pltpu.VMEM(square, BF),
        ]
        + pair_scratch(batches, gram_rows, width, kind)
        + pair_scratch(batches, head_rows, channels, head_kind)
        + [pltpu.SemaphoreType.DMA((2, max(chips, 4)))] * 2
        + [pltpu.SemaphoreType.DMA((tasks, chips))] * 2
        + [pltpu.SemaphoreType.DMA((tasks + 1, chips))] * 2
        + [pltpu.SemaphoreType.DMA((8,)), pltpu.SemaphoreType.DMA((2,))],
        6,
        60,
        flops=50000 * MIB,
        places_out="hhvv",
    )
    outs = [shape(a.shape, F32) for a in (*rows, *matrices)]
    hbm = pl.BlockSpec(memory_space=pltpu.HBM)
    count = trunk_total + head_total
    return pl.pallas_call(
        renew_body,
        out_shape=tuple(outs),
        in_specs=[hbm] * 2 + [VMEM_SPEC] * 6,
        out_specs=tuple(hbm for _ in outs),
        scratch_shapes=[pltpu.VMEM(square, F32)] * 3
        + [pltpu.SemaphoreType.DMA((8 + 2 * (channels // PANEL),))]
        + [pltpu.VMEM((PANEL, 2 * PANEL), F32)] * count
        + [pltpu.VMEM((PANEL, PANEL), F32)] * count,
        compiler_params=pltpu.CompilerParams(vmem_limit_bytes=60 * MIB),
        cost_estimate=pl.CostEstimate(
            flops=60000 * MIB, bytes_accessed=64 * MIB, transcendentals=0
        ),
    )(*made, *matrices)


def local(
    tasks,
    batches,
    images,
    image_small,
    pool_index,
    row_slot,
    trunk_weight,
    trunk_mean_grad,
    trunk_mean_square,
    trunk_statistic,
    trunk_basis,
    head_weight,
    head_mean_grad,
    head_mean_square,
    head_statistic,
    head_basis,
    trunk_gain,
    trunk_offset,
    trunk_norm_mean_grad,
    trunk_norm_mean_square,
    head_gain,
    head_offset,
    head_norm_mean_grad,
    head_norm_mean_square,
    cotangent,
):
    number, height, breadth, channels = images.shape
    pixels = height * breadth
    tap_rows = 9 * channels
    shown = tasks * number
    geometry = (shown, height, breadth)
    task = lax.axis_index("task")
    batch = lax.axis_index("batch")
    width = channels // tasks

    def quarter(values):
        return lax.dynamic_slice_in_dim(values, task * width, width, values.ndim - 1)

    def inside(flags):
        row_limit = jnp.where(flags > 0, height // 2, height)[:, None, None]
        col_limit = jnp.where(flags > 0, breadth // 2, breadth)[:, None, None]
        return (jnp.arange(height, dtype=jnp.int32)[None, :, None] < row_limit) & (
            jnp.arange(breadth, dtype=jnp.int32)[None, None, :] < col_limit
        )

    slots = lax.all_gather(quarter(trunk_weight).astype(BF), "batch", axis=0, tiled=True)
    head_rows = lax.all_gather(head_weight.astype(BF), "batch", axis=1, tiled=True)[0]
    kinds = jnp.concatenate([image_small, pool_index.reshape(-1)])
    kinds = lax.all_gather(kinds, "task", axis=0, tiled=True).reshape(tasks, -1)
    small = kinds[:, :number].reshape(-1)
    cells = kinds[:, number:].reshape(shown, height // 2, 1, breadth // 2, 1)
    cell = 2 * jnp.arange(2, dtype=jnp.int32)[:, None, None] + jnp.arange(2, dtype=jnp.int32)
    choose = (cells == cell).reshape(shown, height, breadth) & inside(small)
    choose = choose.astype(F32)
    choose_row = choose.reshape(shown, 1, pixels)
    choose = choose.reshape(shown * pixels, 1)
    masked = (images * inside(image_small)[..., None].astype(BF)).reshape(number * pixels, channels)
    x = gather_over("task", tasks, (masked,), (0,), 4)[0]
    enc_taps, dec_taps = to_taps(row_slot, slots, channels)

    local_rows = trunk_weight.shape[0]
    slot_ids = batch * local_rows + jnp.arange(local_rows, dtype=jnp.int32)
    decoded = jnp.any(row_slot[tap_rows:][None, :] == slot_ids[:, None], axis=1)
    trunk_onehot = jnp.stack([~decoded, decoded], axis=1).astype(F32)
    x, trunk_onehot = lax.optimization_barrier((x, trunk_onehot))

    scales = quarter(jnp.stack([trunk_gain, trunk_offset], axis=1)).reshape(4, width)
    enc_totals, dec_totals, features, *kept = trunk_forward(
        geometry, tasks, batches, small, x, enc_taps, dec_taps, scales, choose
    )
    head_scales = jnp.stack([head_gain[0], head_offset[0]], axis=1).reshape(6, channels)
    pooled, head_grads, upstream, head_sums = head(
        geometry, tasks, batches, small, features, head_rows,
        cotangent.reshape(shown, pixels // 4, channels), head_scales, enc_totals,
    )
    task_features = pooled.reshape(cotangent.shape)
    enc_grad, dec_grad, flow, trunk_sums, head_owned = trunk_backward(
        geometry, tasks, batches, small, upstream, enc_totals, dec_totals, scales, choose_row,
        head_grads, kept,
    )
    input_grad, trunk_owned, trunk_part, norm_sums = collect(
        tasks, batches, to_slots(row_slot, enc_grad, dec_grad), flow, trunk_sums
    )
    input_grad = input_grad.reshape(images.shape)

    head_local = head_weight.shape[1]
    head_ids = batch * head_local + jnp.arange(head_local, dtype=jnp.int32)
    head_owner = jnp.minimum(head_ids // channels, 2)
    head_onehot = (head_owner[:, None] == jnp.arange(3, dtype=jnp.int32)).astype(F32)
    (
        trunk_weight_new, trunk_one_new, trunk_two_new,
        head_weight_new, head_one_new, head_two_new,
        trunk_stat_new, head_stat_new, trunk_basis_new, head_basis_new,
    ) = finish(
        tasks, batches,
        (trunk_owned, trunk_part, trunk_onehot, head_owned, head_onehot),
        (trunk_weight, trunk_mean_grad, trunk_mean_square,
         head_weight[0], head_mean_grad[0], head_mean_square[0]),
        (trunk_statistic, head_statistic[0], trunk_basis, head_basis[0]),
    )

    trunk_norm = jnp.stack([trunk_gain, trunk_offset], axis=1)
    trunk_norm_grad = norm_sums[:4].reshape(2, 2, channels)[:, ::-1]
    trunk_norm_one, trunk_norm_two, trunk_direction = adam(
        trunk_norm_grad, trunk_norm_mean_grad, trunk_norm_mean_square
    )
    head_norm = jnp.stack([head_gain, head_offset], axis=2)
    head_norm_grad = head_sums[:6].reshape(1, 3, 2, channels)[:, :, ::-1]
    head_norm_one, head_norm_two, head_direction = adam(
        head_norm_grad, head_norm_mean_grad, head_norm_mean_square
    )
    return (
        task_features,
        input_grad,
        trunk_weight_new,
        trunk_one_new,
        trunk_two_new,
        trunk_stat_new,
        trunk_basis_new,
        head_weight_new[None],
        head_one_new[None],
        head_two_new[None],
        head_stat_new[None],
        head_basis_new[None],
        trunk_norm - LEARN_NORM * trunk_direction,
        trunk_norm_one,
        trunk_norm_two,
        head_norm - LEARN_NORM * head_direction,
        head_norm_one,
        head_norm_two,
    )


def solution(mesh):
    placed = (
        P(("task", "batch"), None, None, None),
        P(("task", "batch")),
        P(("task", "batch"), None, None),
        P(),
        P("batch", None),
        P("batch", None),
        P("batch", None),
        P(),
        P(),
        P("task", "batch", None),
        P("task", "batch", None),
        P("task", "batch", None),
        P("task", None, None, None),
        P("task", None, None, None),
        P(),
        P(),
        P(),
        P(),
        P("task", None, None),
        P("task", None, None),
        P("task", None, None, None),
        P("task", None, None, None),
        P("task", None, "batch", None, None, None),
    )
    return jax.shard_map(
        functools.partial(local, mesh.shape["task"], mesh.shape["batch"]),
        mesh=mesh,
        in_specs=placed,
        out_specs=(
            P("task", None, "batch", None, None, None),
            P(("task", "batch"), None, None, None),
            P("batch", None),
            P("batch", None),
            P("batch", None),
            P(),
            P(),
            P("task", "batch", None),
            P("task", "batch", None),
            P("task", "batch", None),
            P("task", None, None, None),
            P("task", None, None, None),
            P(),
            P(),
            P(),
            P("task", None, None, None),
            P("task", None, None, None),
            P("task", None, None, None),
        ),
        check_vma=False,
    )
```

profile of v0, /device:TPU:0, one launch (start us, length us, event | category | flops | bytes accessed | tf_op | source)
XLA Modules:
  0.0 751.2 jit_solution(8984472054651336086)
XLA Ops:
  7.2 0.0 copy-start.15
  7.2 0.0 all-gather.3.cloned.1.call-start
  7.3 1.9 dynamic-slice_convert_fusion
  9.1 0.0 all-gather.3.cloned.1.call-update
  9.2 0.0 all-gather.5.cloned.1.call-start
  9.2 2.3 convert_element_type.43
  11.5 0.0 all-gather.5.cloned.1.call-update
  11.6 0.1 reshape.364
  12.3 0.6 dynamic-slice
  13.6 0.2 add_dynamic-update-slice_fusion
  13.8 8.8 %all-reduce = s32[436]{0:T(512)S(1)} all-reduce(s32[436]{0:T(512)S(1)} %add_dynamic-update-slice_fusion), channel_id=1, replica_groups=mesh['task'=4,'batch'=8] {'task'}, use_global_device_ids=true, to_apply=%add | all-reduce | flops 436 | bytes 3488
  22.6 0.1 reshape.365
  22.7 0.1 slice.17
  22.7 0.1 slice_reduce_fusion.small
  22.9 0.1 iota_compare_fusion.1
  22.9 0.1 iota_compare_fusion.2
  23.0 0.1 broadcast_and_fusion
  23.1 0.4 and.98
  23.5 0.0 copy-start.6
  23.5 0.0 copy-start.7
  23.5 0.1 and.99
  23.6 0.1 iota_add_fusion.2
  23.7 0.1 eq.81
  23.8 0.1 eq.86
  24.0 0.1 and_convert_fusion.2
  24.1 0.9 broadcast_multiply_fusion
  25.0 22.7 %shard_map.358.x = bf16[1728,512]{1,0:T(8,128)(2,1)} custom-call(bf16[432,512]{1,0:T(8,128)(2,1)} %bitcast.27), custom_call_target="tpu_custom_call" | custom-call | bytes 2211840 | tf_op jit(solution)/shard_map/pallas_call | solution.py:837
  47.7 0.0 copy-start.4
  47.7 0.0 copy-start.5
  47.7 2.8 compare_reduce_fusion
  50.6 0.3 copy.114
  50.9 0.9 convert_element_type.40.owners
  51.8 0.6 copy.115
  52.4 0.1 eq.77
  52.5 0.1 copy.116
  52.6 0.1 eq.78.clone
  52.8 0.2 eq.79
  53.0 0.1 eq.83
  53.1 0.4 copy.118
  53.5 0.8 copy.120.cotangent
  54.4 0.6 reshape.370.scales
  55.0 0.1 eq.78
  55.1 0.1 copy.122
  55.2 0.6 and_convert_fusion.1.choose_row
  55.8 0.9 fusion.head_owners
  56.7 1.0 and_convert_fusion.choose
  57.8 12.2 %shard_map.359 = (bf16[512,1152]{1,0:T(8,128)(2,1)}, bf16[512,1152]{1,0:T(8,128)(2,1)}) custom-call(s32[9216]{0:T(1024)} %index.3, bf16[9216,128]{1,0:T(8,128)(2,1)} %all-gather.3.cloned.1.call-done.slots), custom_call_target="tpu_custom_call" | custom-call | flops 10485760000 | bytes 4755456 | tf_op jit(solution)/shard_map/pallas_call | solution.py:32
  70.0 52.2 %shard_map.360 = (f32[8,128]{1,0:T(8,128)}, f32[8,128]{1,0:T(8,128)}, bf16[1728,512]{1,0:T(8,128)(2,1)}, bf16[1728,512]{1,0:T(8,128)(2,1)}, bf16[512,1152]{1,0:T...) custom-call(s32[4]{0:T(128)} %copy-done.14, ...), custom_call_target="tpu_custom_call" | custom-call | flops 4076863488 | bytes 13583120 | tf_op jit(solution)/shard_map/pallas_call | solution.py:229
  122.2 0.0 all-gather.5.cloned.1.call-done
  122.2 86.0 %shard_map.361 = (bf16[4,108,512]{2,1,0:T(8,128)(2,1)}, bf16[5632,512]{1,0:T(8,128)(2,1)}, f32[1728,128]{1,0:T(8,128)}, f32[8,512]{1,0:T(8,128)}) custom-call(s32[4]{0:T(128)} %copy-done.14, bf16[1728,512]{1,0:T(8,128)(2,1)} %get-tuple-element.61.features, bf16[5632,512]{1,0:T(8,128)(2,1)} %bitcast.44, bf16[4,108,512]{2,1,0:T(8,128)(2,1)} %copy.120.cotangent, ...), custom_call_target="tpu_custom_call" | custom-call | flops 29896998912 | bytes 15106064 | tf_op jit(solution)/shard_map/pallas_call | solution.py:229
  208.3 2.1 copy.121
  210.4 69.1 %shard_map.362 = (f32[512,1152]{1,0:T(8,128)}, f32[512,1152]{1,0:T(8,128)}, bf16[1728,512]{1,0:T(8,128)(2,1)}, f32[8,128]{1,0:T(8,128)}, bf16[704,512]{1,0:T(8,128)(2,1)}) custom-call(s32[4]{0:T(128)} %copy-done.14, f32[1728,128]{1,0:T(8,128)} %get-tuple-element.64.upstream, f32[8,128]{1,0:T(8,128)} %get-tuple-element.62.counts.enc_totals, ...), custom_call_target="tpu_custom_call" | custom-call | flops 8153726976 | bytes 21549840 | tf_op jit(solution)/shard_map/pallas_call | solution.py:229
  279.5 12.6 %shard_map.363.slots = bf16[9216,128]{1,0:T(8,128)(2,1)} custom-call(s32[9216]{0:T(1024)} %index.3, f32[512,1152]{1,0:T(8,128)} %get-tuple-element.73.enc, f32[512,1152]{1,0:T(8,128)} %get-tuple-element.74.dec), custom_call_target="tpu_custom_call" | custom-call | bytes 7114752 | tf_op jit(solution)/shard_map/pallas_call | solution.py:32
  292.1 0.0 copy-start.10
  292.1 42.8 %shard_map.364 = (f32[432,512]{1,0:T(8,128)}, bf16[1152,512]{1,0:T(8,128)(2,1)}, bf16[1152,128]{1,0:T(8,128)(2,1)}, f32[8,512]{1,0:T(8,128)}) custom-call(bf16[9216,128]{1,0:T(8,128)(2,1)} %shard_map.363.slots, bf16[1728,512]{1,0:T(8,128)(2,1)} %get-tuple-element.75.flow, f32[8,128]{1,0:T(8,128)} %get-tuple-element.76.sums), custom_call_target="tpu_custom_call" | custom-call | flops 20971520000 | bytes 6508544 | tf_op jit(solution)/shard_map/pallas_call | solution.py:229
  334.9 0.7 slice.18
  335.8 0.6 copy.128
  336.4 0.6 copy.129
  337.0 0.6 copy.130
  337.6 0.2 rev.7
  337.8 0.7 maximum_subtract_fusion
  338.4 53.0 %shard_map.365 = (f32[3,1152,512]{2,1,0:T(8,128)}, f32[3,704,512]{2,1,0:T(8,128)}, bf16[1024,512]{1,0:T(8,128)(2,1)}, bf16[1536,512]{1,0:T(8,128)(2,1)}) custom-call(bf16[1152,512]{1,0:T(8,128)(2,1)} %get-tuple-element.78.grad, bf16[1152,128]{1,0:T(8,128)(2,1)} %get-tuple-element.79.part, f32[1152,2]{1,0:T(8,128)} %convert_element_type.40.owners, ...), custom_call_target="tpu_custom_call" | custom-call | flops 52428800000 | bytes 32883968 | tf_op jit(solution)/shard_map/pallas_call | solution.py:229
  391.4 351.6 %shard_map.366 = (f32[1152,512]{1,0:T(8,128)}, f32[1152,512]{1,0:T(8,128)}, f32[1152,512]{1,0:T(8,128)}, f32[704,512]{1,0:T(8,128)}, f32[704,512]{1,0:T(8,128)},...) custom-call(f32[3,1152,512]{2,1,0:T(8,128)} %get-tuple-element.82.st, ...), custom_call_target="tpu_custom_call" | custom-call | flops 62914560000 | bytes 67108864 | tf_op jit(solution)/shard_map/pallas_call | solution.py:1553
  743.0 0.9 copy.143
  (48 shorter events, 0.3 us)
Async XLA Ops:
  7.2 5.1 copy-start.15
  7.2 4.3 copy-start.13
  7.2 16.9 %copy-start.1 = (bf16[1,18,24,512]{3,2,1,0:T(8,128)(2,1)S(1)}, bf16[1,18,24,512]{3,2,1,0:T(8,128)(2,1)}, u32[]{:S(2)}) copy-start(bf16[1,18,24,512]{3,2,1,0:T(8,128)(2,1)} %param.23) | copy-start | bytes 1327108
  7.2 50.5 %all-gather.3.cloned.1.call-start = ((), (), s32[]{:S(2)}) async-start(), calls=%async_computation | async-start | bytes 2654208 | tf_op jit(solution)/shard_map/all_gather | solution.py:1615
  9.2 113.1 %all-gather.5.cloned.1.call-start = ((), (), s32[]{:S(2)}) async-start(), calls=%async_computation.1 | async-start | bytes 6488064 | tf_op jit(solution)/shard_map/all_gather | solution.py:1616
  11.5 36.1 %copy-start.3 = (s32[9216]{0:T(1024)S(1)}, s32[9216]{0:T(1024)}, u32[]{:S(2)}) copy-start(s32[9216]{0:T(1024)} %index.3) | copy-start | bytes 110596
  22.9 28.9 %copy-start.14 = (s32[4]{0:T(128)}, s32[4]{0:T(128)S(1)}, u32[]{:S(2)}) copy-start(s32[4]{0:T(128)S(1)} %slice_reduce_fusion.small) | copy-start | bytes 52
  23.5 28.3 %copy-start.6 = (f32[2,512]{1,0:T(2,128)S(1)}, f32[2,512]{1,0:T(2,128)}, u32[]{:S(2)}) copy-start(f32[2,512]{1,0:T(2,128)} %param.37) | copy-start | bytes 12292
  23.5 28.3 %copy-start.7 = (f32[2,512]{1,0:T(2,128)S(1)}, f32[2,512]{1,0:T(2,128)}, u32[]{:S(2)}) copy-start(f32[2,512]{1,0:T(2,128)} %param.38) | copy-start | bytes 12292
  25.0 28.6 %copy-start.2 = (bf16[1,4,1,9,12,512]{5,1,4,3,2,0:T(4,128)(2,1)S(1)}, bf16[1,4,1,9,12,512]{5,1,4,3,2,0:T(4,128)(2,1)}, u32[]{:S(2)}) copy-start(bf16[1,4,1,9,12,512]{5,1,4,3,2,0:T(4,128)(2,1)} %param.45) | copy-start | bytes 1327108
  47.7 6.7 copy-start.4
  47.7 6.7 copy-start.5
  292.1 43.6 %copy-start.11 = (f32[2,2,512]{2,1,0:T(2,128)S(1)}, f32[2,2,512]{2,1,0:T(2,128)}, u32[]{:S(2)}) copy-start(f32[2,2,512]{2,1,0:T(2,128)} %param.39) | copy-start | bytes 24580
  292.1 43.6 %copy-start.12 = (f32[2,2,512]{2,1,0:T(2,128)S(1)}, f32[2,2,512]{2,1,0:T(2,128)}, u32[]{:S(2)}) copy-start(f32[2,2,512]{2,1,0:T(2,128)} %param.40) | copy-start | bytes 24580
  292.1 45.5 %copy-start.8 = (f32[8,512]{1,0:T(8,128)S(1)}, f32[8,512]{1,0:T(8,128)}, u32[]{:S(2)}) copy-start(f32[8,512]{1,0:T(8,128)} %get-tuple-element.97) | copy-start | bytes 49156
  292.1 45.6 %copy-start.9 = (f32[1,3,2,512]{3,2,1,0:T(2,128)S(1)}, f32[1,3,2,512]{3,2,1,0:T(2,128)}, u32[]{:S(2)}) copy-start(f32[1,3,2,512]{3,2,1,0:T(2,128)} %param.43) | copy-start | bytes 36868
  292.1 45.6 %copy-start.10 = (f32[1,3,2,512]{3,2,1,0:T(2,128)S(1)}, f32[1,3,2,512]{3,2,1,0:T(2,128)}, u32[]{:S(2)}) copy-start(f32[1,3,2,512]{3,2,1,0:T(2,128)} %param.44) | copy-start | bytes 36868
  391.4 351.6 %copy-start = (f32[432,512]{1,0:T(8,128)S(1)}, f32[432,512]{1,0:T(8,128)}, u32[]{:S(2)}) copy-start(f32[432,512]{1,0:T(8,128)} %get-tuple-element.77) | copy-start | bytes 2654212
Sparse Core Ops, SparseCore 0:
  10.3 34.3 all-gather.2
  46.9 60.8 all-gather.4
where the time goes:
time: 761 us; the launch traced here: 751 us
  Pallas kernels  702 us (92%)
  between operations  16.2 us (2%)
  local copies, waits for them, and re-layouts  13 us (2%)
  other arithmetic  10.8 us (1%)
  blocking collectives  8.82 us (1%)
    pallas_call x1, Pallas kernels, finish(): pl.pallas_call(renew_body, out_shape=tuple(outs), in_specs=[hbm] * 2 + [V...  352 us
    pallas_call x5, Pallas kernels, exchange_kernel(): pl.pallas_call(body, out_shape=tuple(outs), in_specs=[SPECS[s] for s in s...  303 us
    pallas_call x2, Pallas kernels, run(): pl.pallas_call(body, out_shape=tuple(outs), in_specs=[SMEM_SPEC if s == '...  24.8 us
    pallas_call x1, Pallas kernels, exchange(): pl.pallas_call(body, out_shape=tuple(outs), in_specs=[VMEM_SPEC] * len(ar...  22.7 us
  transfers between devices with their start and end apart: 2, of which 0 were waited for; matrix products, arithmetic and copies ran while one was open for 2% of the time, Pallas kernels for 12%

commit v1 on v0

--- a/solution.py
+++ b/solution.py
@@ -635,6 +635,9 @@
     )
 
 
+SUM_IN_KERNEL = False
+
+
 def trunk_backward_body(
     geometry, tasks, batches, summing,
     small, upstream, enc_totals, dec_totals, scales, choose_row, *rest,
@@ -788,7 +791,7 @@
     width = channels // tasks
     windows = window_count(height, breadth)
     head_rows = head_grads.shape[0]
-    summing = head_rows % (16 * batches) == 0
+    summing = SUM_IN_KERNEL and head_rows % (16 * batches) == 0
     outs = [
         shape(enc_taps.shape, F32),
         shape(dec_taps.shape, F32),
@@ -832,82 +835,6 @@
     return *made, lax.psum_scatter(head_grads, "batch", scatter_dimension=0, tiled=True)
 
 
-def exchange(body, outs, args, scratch, identity, vmem=60):
-    size = sum(o.size * o.dtype.itemsize for o in outs) + sum(a.size * a.dtype.itemsize for a in args)
-    return pl.pallas_call(
-        body,
-        out_shape=tuple(outs),
-        in_specs=[VMEM_SPEC] * len(args),
-        out_specs=tuple(VMEM_SPEC for _ in outs),
-        scratch_shapes=list(scratch),
-        compiler_params=pltpu.CompilerParams(
-            vmem_limit_bytes=vmem * MIB, collective_id=identity, has_side_effects=True
-        ),
-        cost_estimate=pl.CostEstimate(flops=0, bytes_accessed=size, transcendentals=0),
-    )(*args)
-
-
-def block_of(ref, place, size, dim):
-    length = ref.shape[dim] // size
-    start = place * length
-    if dim == 0:
-        return ref.at[pl.ds(pl.multiple_of(start, 8), length), :]
-    return ref.at[:, pl.ds(pl.multiple_of(start, 128), length)]
-
-
-def gather_body(axis, size, dims, *refs):
-    count = len(dims)
-    sources, targets = refs[:count], refs[count : 2 * count]
-    sends, receives, own = refs[2 * count :]
-    greet(((axis, size),))
-    me = lax.axis_index(axis)
-    copies = []
-    for k in range(count):
-        mine = block_of(targets[k], me, size, dims[k])
-        for step in range(1, size):
-            peer = lax.rem(me + step, size)
-            copy = remote(sources[k], mine, sends.at[k, step], receives.at[k, me], peer, axis)
-            copy.start()
-            copies.append(copy)
-    locals_ = []
-    for k in range(count):
-        mine = block_of(targets[k], me, size, dims[k])
-        copy = pltpu.make_async_copy(sources[k], mine, own.at[k])
-        copy.start()
-        locals_.append(copy)
-    for copy in locals_:
-        copy.wait()
-    for k in range(count):
-        for step in range(1, size):
-            peer = lax.rem(me + size - step, size)
-            theirs = block_of(targets[k], peer, size, dims[k])
-            remote(
-                sources[k], theirs, sends.at[k, step], receives.at[k, peer], peer, axis
-            ).wait_recv()
-    for copy in copies:
-        copy.wait_send()
-
-
-def gather_over(axis, size, arrays, dims, identity):
-    outs = []
-    for x, dim in zip(arrays, dims):
-        full = list(x.shape)
-        full[dim] *= size
-        outs.append(shape(full, x.dtype))
-    count = len(arrays)
-    return exchange(
-        functools.partial(gather_body, axis, size, tuple(dims)),
-        outs,
-        arrays,
-        [
-            pltpu.SemaphoreType.DMA((count, size)),
-            pltpu.SemaphoreType.DMA((count, size)),
-            pltpu.SemaphoreType.DMA((count,)),
-        ],
-        identity,
-    )
-
-
 def to_taps_body(index, slots, enc, dec, wide, tap):
     count = slots.shape[0]
     channels = enc.shape[0]
@@ -1165,6 +1092,102 @@
                 pass_on(way).wait_send()
 
     return start, relay, settle, drain
+
+
+def arrive_body(
+    tasks, batches,
+    image, info, weight,
+    slots, x, infos,
+    raw, raw_loaded, x_send, x_receive, info_send, info_receive,
+    chip_send, chip_receive, pair_send, pair_receive, own,
+):
+    task = lax.axis_index("task")
+    place, core, chips = pair_place(batches)
+    count, width = raw.shape
+    load = pltpu.make_async_copy(weight.at[:, columns_of(task, width)], raw, raw_loaded)
+    load.start()
+    greet_pairs(tasks, batches)
+
+    def task_copy(source, target, sends, receives, step, incoming=False):
+        peer = lax.rem(task + (tasks - step if incoming else step), tasks)
+        home = peer if incoming else task
+        return remote(source, block_rows(target, home, source.shape[0]), sends.at[step],
+                      receives.at[step], peer, "task")
+
+    def moves(step, incoming=False):
+        return (
+            task_copy(info, infos, info_send, info_receive, step, incoming),
+            task_copy(image, x, x_send, x_receive, step, incoming),
+        )
+
+    def block(chip):
+        return block_rows(slots, 2 * chip + core, count)
+
+    def pair_copy(hop, incoming=False):
+        chip = lax.rem(place + chips - hop, chips)
+        ref = block_rows(slots, 2 * chip + (1 - core if incoming else core), count)
+        return remote(ref, ref, pair_send.at[hop], pair_receive.at[hop], 2 * place + 1 - core, "batch")
+
+    start, relay, settle, drain = chip_spread(batches, block, chip_send, chip_receive)
+    load.wait()
+    block(place)[...] = raw[...].astype(BF)
+    start()
+    pair_copy(0).start()
+    for step in range(1, tasks):
+        for copy in moves(step):
+            copy.start()
+    locals_ = [
+        pltpu.make_async_copy(image, block_rows(x, task, image.shape[0]), own.at[0]),
+        pltpu.make_async_copy(info, block_rows(infos, task, info.shape[0]), own.at[1]),
+    ]
+    for copy in locals_:
+        copy.start()
+    relay()
+    if chips == 4 and count % 32 == 0:
+        pair_copy(1).start()
+        pair_copy(3).start()
+        settle()
+        pair_copy(2).start()
+    else:
+        settle()
+        for hop in range(1, chips):
+            pair_copy(hop).start()
+    for copy in locals_:
+        copy.wait()
+    for step in range(1, tasks):
+        for copy in moves(step, True):
+            copy.wait_recv()
+    for hop in range(chips):
+        pair_copy(hop, True).wait_recv()
+    for step in range(1, tasks):
+        for copy in moves(step):
+            copy.wait_send()
+    for hop in range(chips):
+        pair_copy(hop).wait_send()
+    drain()
+
+
+def arrive(tasks, batches, image, info, weight):
+    count, channels = weight.shape
+    width = channels // tasks
+    chips = batches // 2
+    return exchange_kernel(
+        functools.partial(arrive_body, tasks, batches),
+        [
+            shape((count * batches, width), BF),
+            shape((image.shape[0] * tasks, channels), BF),
+            shape((info.shape[0] * tasks, info.shape[1]), F32),
+        ],
+        "vvh",
+        (image, info, weight),
+        [pltpu.VMEM((count, width), F32), pltpu.SemaphoreType.DMA]
+        + [pltpu.SemaphoreType.DMA((tasks,))] * 4
+        + [pltpu.SemaphoreType.DMA((max(chips, 4),))] * 4
+        + [pltpu.SemaphoreType.DMA((2,))],
+        4,
+        60,
+        flops=20000 * MIB,
+    )
 
 
 def collect_body(
@@ -1471,17 +1494,21 @@
     state, head_state, grams, head_grams, stat, head_stat, basis, head_basis,
     weight_new, one_new, two_new, head_weight_new, head_one_new, head_two_new,
     stat_new, head_stat_new, basis_new, head_basis_new,
-    stats, product, made, save, *work,
+    stats, product, made, held, head_held, load, save, *work,
 ):
     trunk_total, head_total = stat.shape[0], head_stat.shape[0]
     channels = stat.shape[1]
     count = trunk_total + head_total
     tables, inverses = work[:count], work[count:]
-    sources = [state.at[k] for k in range(3)] + [head_state.at[k] for k in range(3)]
+    loads = [
+        pltpu.make_async_copy(state, held, load.at[0]),
+        pltpu.make_async_copy(head_state, head_held, load.at[1]),
+    ]
+    for copy in loads:
+        copy.start()
+    sources = [held.at[k] for k in range(3)] + [head_held.at[k] for k in range(3)]
     targets = [weight_new, one_new, two_new, head_weight_new, head_one_new, head_two_new]
     saves = [pltpu.make_async_copy(a, b, save.at[k]) for k, (a, b) in enumerate(zip(sources, targets))]
-    for copy in saves:
-        copy.start()
     for m in range(count):
         first = m < trunk_total
         place = m if first else m - trunk_total
@@ -1494,6 +1521,10 @@
         copy = pltpu.make_async_copy(stats.at[pl.ds(begin, size)], out, save.at[len(saves)])
         copy.start()
         saves.append(copy)
+    for copy in loads:
+        copy.wait()
+    for copy in saves[:6]:
+        copy.start()
     for k in range(channels // PANEL):
         renew_panel(k, product, made, tables, inverses)
         cut = pl.ds(k * PANEL, PANEL)
@@ -1556,6 +1587,8 @@
         in_specs=[hbm] * 2 + [VMEM_SPEC] * 6,
         out_specs=tuple(hbm for _ in outs),
         scratch_shapes=[pltpu.VMEM(square, F32)] * 3
+        + [pltpu.VMEM(made[0].shape, F32), pltpu.VMEM(made[1].shape, F32)]
+        + [pltpu.SemaphoreType.DMA((2,))]
         + [pltpu.SemaphoreType.DMA((8 + 2 * (channels // PANEL),))]
         + [pltpu.VMEM((PANEL, 2 * PANEL), F32)] * count
         + [pltpu.VMEM((PANEL, PANEL), F32)] * count,
@@ -1612,19 +1645,22 @@
             jnp.arange(breadth, dtype=jnp.int32)[None, None, :] < col_limit
         )
 
-    slots = lax.all_gather(quarter(trunk_weight).astype(BF), "batch", axis=0, tiled=True)
-    head_rows = lax.all_gather(head_weight.astype(BF), "batch", axis=1, tiled=True)[0]
-    kinds = jnp.concatenate([image_small, pool_index.reshape(-1)])
-    kinds = lax.all_gather(kinds, "task", axis=0, tiled=True).reshape(tasks, -1)
-    small = kinds[:, :number].reshape(-1)
-    cells = kinds[:, number:].reshape(shown, height // 2, 1, breadth // 2, 1)
     cell = 2 * jnp.arange(2, dtype=jnp.int32)[:, None, None] + jnp.arange(2, dtype=jnp.int32)
-    choose = (cells == cell).reshape(shown, height, breadth) & inside(small)
-    choose = choose.astype(F32)
-    choose_row = choose.reshape(shown, 1, pixels)
-    choose = choose.reshape(shown * pixels, 1)
-    masked = (images * inside(image_small)[..., None].astype(BF)).reshape(number * pixels, channels)
-    x = gather_over("task", tasks, (masked,), (0,), 4)[0]
+    cells = pool_index.reshape(number, height // 2, 1, breadth // 2, 1)
+    valid = inside(image_small)
+    chosen = ((cells == cell).reshape(number, height, breadth) & valid).reshape(number, pixels)
+    info = jnp.zeros((8 * number, channels), F32)
+    info = info.at[::8, :pixels].set(chosen.astype(F32))
+    info = info.at[1::8, 0].set(image_small.astype(F32))
+    masked = (images * valid[..., None].astype(BF)).reshape(number * pixels, channels)
+    slots, x, infos = arrive(tasks, batches, masked, info, trunk_weight)
+    head_low = head_weight.astype(BF)
+    slots, head_low = lax.optimization_barrier((slots, head_low))
+    head_rows = lax.all_gather(head_low, "batch", axis=1, tiled=True)[0]
+    infos = infos.reshape(shown, 8, channels)
+    small = infos[:, 1, 0].astype(jnp.int32)
+    choose_row = infos[:, :1, :pixels]
+    choose = choose_row.reshape(shown * pixels, 1)
     enc_taps, dec_taps = to_taps(row_slot, slots, channels)
 
     local_rows = trunk_weight.shape[0]

time: 761 us -> 433 us (0.57)
  Pallas kernels: 702 us -> 390 us
  blocking collectives: 8.82 us -> 0 us
    pallas_call x1, Pallas kernels: 352 us -> 62 us  [finish(): pl.pallas_call(renew_body, out_shape=tuple(outs), in_specs=[hbm] * 2 + [V...]
    pallas_call x1 -> x0, Pallas kernels: 22.7 us -> none  [exchange(): pl.pallas_call(body, out_shape=tuple(outs), in_specs=[VMEM_SPEC] * len(ar...]
    unnamed x1 -> x0, blocking collectives: 8.82 us -> none
    pallas_call x5 -> x6, Pallas kernels: 303 us -> 303 us  [exchange_kernel(): pl.pallas_call(body, out_shape=tuple(outs), in_specs=[SPECS[s] for s in s...]
  transfers between devices with their start and end apart: 2 -> 2, of which waited for: 0 -> 0; matrix products, arithmetic and copies ran while one was open for 2% -> 4% of each run, Pallas kernels for 12% -> 38%
where the time goes in v1:
time: 433 us; the launch traced here: 428 us
  Pallas kernels  390 us (90%)
  between operations  15.3 us (4%)
  local copies, waits for them, and re-layouts  11.9 us (3%)
  other arithmetic  10.2 us (2%)
    pallas_call x6, Pallas kernels, exchange_kernel(): pl.pallas_call(body, out_shape=tuple(outs), in_specs=[SPECS[s] for s in s...  303 us
    pallas_call x1, Pallas kernels, finish(): pl.pallas_call(renew_body, out_shape=tuple(outs), in_specs=[hbm] * 2 + [V...  62 us
    pallas_call x2, Pallas kernels, run(): pl.pallas_call(body, out_shape=tuple(outs), in_specs=[SMEM_SPEC if s == '...  25.4 us
  transfers between devices with their start and end apart: 2, of which 0 were waited for; matrix products, arithmetic and copies ran while one was open for 4% of the time, Pallas kernels for 38%

profile of v1, /device:TPU:0, one launch (start us, length us, event | category | flops | bytes accessed | tf_op | source)
XLA Modules:
  0.0 428.0 jit_solution(3862712642651966482)
XLA Ops:
  7.2 0.0 copy-start.2
  7.2 0.0 all-gather.2.cloned.1.call-start
  8.0 0.1 iota_add_fusion.2
  8.1 0.7 copy.88
  8.7 0.1 broadcast_compare_fusion
  8.8 0.1 eq.62
  9.0 0.1 and_convert_fusion
  9.1 0.1 and.78
  9.1 0.1 and.79
  9.3 0.1 and.80
  9.4 2.3 convert_element_type.41
  11.7 0.0 copy-done.2
  11.7 0.9 broadcast_multiply_fusion
  12.6 0.0 copy-start.10
  12.6 0.6 copy-done.10
  13.2 30.6 %shard_map.358 = (bf16[9216,128]{1,0:T(8,128)(2,1)}, bf16[1728,512]{1,0:T(8,128)(2,1)}, f32[32,512]{1,0:T(8,128)}) custom-call(bf16[432,512]{1,0:T(8,128)(2,1)} %bitcast.36, f32[8,512]{1,0:T(8,128)} %copy-done.10, f32[1152,512]{1,0:T(8,128)} %weight.3), custom_call_target="tpu_custom_call" | custom-call | flops 20971520000 | bytes 7012352 | tf_op jit(solution)/shard_map/pallas_call | solution.py:229
  43.9 0.0 copy-start.3
  43.9 0.0 copy-start.5
  43.9 0.0 copy-start.6
  43.9 0.0 all-gather.2.cloned.1.call-update
  43.9 0.0 reduce-scatter.2.cloned.1.call-start
  44.0 0.0 copy-done.4
  44.0 2.8 compare_reduce_fusion
  46.9 0.3 copy.67
  47.2 0.9 convert_element_type.40.owners
  48.1 0.0 copy-done.7
  48.1 0.0 copy-done.8
  48.1 0.6 copy.68
  48.7 1.4 fusion.12
  50.1 1.3 reshape.340.choose
  51.4 0.0 copy-done.3
  51.4 0.8 copy.70.cotangent
  52.2 0.0 copy-done.5
  52.2 0.0 copy-done.6
  52.2 0.6 reshape.335.scales
  52.9 1.4 fusion.9.small
  54.3 12.8 %shard_map.359 = (bf16[512,1152]{1,0:T(8,128)(2,1)}, bf16[512,1152]{1,0:T(8,128)(2,1)}) custom-call(s32[9216]{0:T(1024)} %index.3, bf16[9216,128]{1,0:T(8,128)(2,1)} %get-tuple-element.90.slots), custom_call_target="tpu_custom_call" | custom-call | flops 10485760000 | bytes 4755456 | tf_op jit(solution)/shard_map/pallas_call | solution.py:32
  67.0 51.8 %shard_map.360 = (f32[8,128]{1,0:T(8,128)}, f32[8,128]{1,0:T(8,128)}, bf16[1728,512]{1,0:T(8,128)(2,1)}, bf16[1728,512]{1,0:T(8,128)(2,1)}, bf16[512,1152]{1,0:T...) custom-call(s32[4]{0:T(128)} %fusion.9.small, ...), custom_call_target="tpu_custom_call" | custom-call | flops 4076863488 | bytes 13583120 | tf_op jit(solution)/shard_map/pallas_call | solution.py:229
  118.8 0.0 all-gather.2.cloned.1.call-done
  118.8 85.1 %shard_map.361 = (bf16[4,108,512]{2,1,0:T(8,128)(2,1)}, bf16[5632,512]{1,0:T(8,128)(2,1)}, f32[1728,128]{1,0:T(8,128)}, f32[8,512]{1,0:T(8,128)}) custom-call(s32[4]{0:T(128)} %fusion.9.small, bf16[1728,512]{1,0:T(8,128)(2,1)} %get-tuple-element.93.features, bf16[5632,512]{1,0:T(8,128)(2,1)} %bitcast.51, bf16[4,108,512]{2,1,0:T(8,128)(2,1)} %copy.70.cotangent, ...), custom_call_target="tpu_custom_call" | custom-call | flops 29896998912 | bytes 15106064 | tf_op jit(solution)/shard_map/pallas_call | solution.py:229
  204.0 0.0 copy-start.1
  204.0 0.0 reduce-scatter.2.cloned.1.call-update
  204.0 0.9 fusion.head_owners
  204.9 0.1 copy-done.1
  205.0 1.1 copy.71
  206.1 30.7 %shard_map.362 = (f32[512,1152]{1,0:T(8,128)}, f32[512,1152]{1,0:T(8,128)}, bf16[1728,512]{1,0:T(8,128)(2,1)}, f32[8,128]{1,0:T(8,128)}) custom-call(s32[4]{0:T(128)} %fusion.9.small, f32[1728,128]{1,0:T(8,128)} %get-tuple-element.97.upstream, f32[8,128]{1,0:T(8,128)} %get-tuple-element.95.counts.enc_totals, f32[8,128]{1,0:T(8,128)} %get-tuple-element.98.dec_totals, ...), custom_call_target="tpu_custom_call" | custom-call | flops 8153726976 | bytes 15061776 | tf_op jit(solution)/shard_map/pallas_call | solution.py:229
  236.8 12.6 %shard_map.363.slots = bf16[9216,128]{1,0:T(8,128)(2,1)} custom-call(s32[9216]{0:T(1024)} %index.3, f32[512,1152]{1,0:T(8,128)} %get-tuple-element.105.enc, f32[512,1152]{1,0:T(8,128)} %get-tuple-element.106.dec), custom_call_target="tpu_custom_call" | custom-call | bytes 7114752 | tf_op jit(solution)/shard_map/pallas_call | solution.py:32
  249.4 0.0 copy-start.12
  249.4 53.5 %shard_map.364 = (f32[432,512]{1,0:T(8,128)}, bf16[1152,512]{1,0:T(8,128)(2,1)}, bf16[1152,128]{1,0:T(8,128)(2,1)}, f32[8,512]{1,0:T(8,128)}) custom-call(bf16[9216,128]{1,0:T(8,128)(2,1)} %shard_map.363.slots, bf16[1728,512]{1,0:T(8,128)(2,1)} %get-tuple-element.107.flow, f32[8,128]{1,0:T(8,128)} %get-tuple-element.108.sums), custom_call_target="tpu_custom_call" | custom-call | flops 20971520000 | bytes 6508544 | tf_op jit(solution)/shard_map/pallas_call | solution.py:229
  302.9 0.7 slice.53
  303.7 0.0 copy-done.13
  303.7 0.0 copy-done.14
  303.7 0.6 copy.75
  304.4 0.6 copy.76
  305.0 0.6 copy.77
  305.6 0.0 copy-done.9
  305.6 0.4 rev.7
  306.0 0.0 copy-done.11
  306.0 0.0 copy-done.12
  306.0 0.7 maximum_subtract_fusion
  306.6 51.4 %shard_map.365 = (f32[3,1152,512]{2,1,0:T(8,128)}, f32[3,704,512]{2,1,0:T(8,128)}, bf16[1024,512]{1,0:T(8,128)(2,1)}, bf16[1536,512]{1,0:T(8,128)(2,1)}) custom-call(bf16[1152,512]{1,0:T(8,128)(2,1)} %get-tuple-element.110.grad, bf16[1152,128]{1,0:T(8,128)(2,1)} %get-tuple-element.111.part, f32[1152,2]{1,0:T(8,128)} %convert_element_type.40.owners, ...), custom_call_target="tpu_custom_call" | custom-call | flops 52428800000 | bytes 32883968 | tf_op jit(solution)/shard_map/pallas_call | solution.py:229
  358.0 0.0 copy-start
  358.0 62.0 %shard_map.366 = (f32[1152,512]{1,0:T(8,128)}, f32[1152,512]{1,0:T(8,128)}, f32[1152,512]{1,0:T(8,128)}, f32[704,512]{1,0:T(8,128)}, f32[704,512]{1,0:T(8,128)},...) custom-call(f32[3,1152,512]{2,1,0:T(8,128)} %get-tuple-element.114.s, ...), custom_call_target="tpu_custom_call" | custom-call | flops 62914560000 | bytes 67108864 | tf_op jit(solution)/shard_map/pallas_call | solution.py:1584
  420.1 0.9 copy.92
  (28 shorter events, 0.3 us)
Async XLA Ops:
  7.2 4.5 %copy-start.2 = (bf16[1,18,24,512]{3,2,1,0:T(8,128)(2,1)S(1)}, bf16[1,18,24,512]{3,2,1,0:T(8,128)(2,1)}, u32[]{:S(2)}) copy-start(bf16[1,18,24,512]{3,2,1,0:T(8,128)(2,1)} %param.27) | copy-start | bytes 1327108
  7.2 111.6 %all-gather.2.cloned.1.call-start = ((), (), s32[]{:S(2)}) async-start(), calls=%async_computation.1 | async-start | bytes 6488064 | tf_op jit(solution)/shard_map/all_gather | solution.py:1659
  12.6 0.6 copy-start.10
  13.2 30.7 %copy-start.4 = (s32[9216]{0:T(1024)S(1)}, s32[9216]{0:T(1024)}, u32[]{:S(2)}) copy-start(s32[9216]{0:T(1024)} %index.3) | copy-start | bytes 110596
  13.2 34.8 %copy-start.7 = (f32[2,512]{1,0:T(2,128)S(1)}, f32[2,512]{1,0:T(2,128)}, u32[]{:S(2)}) copy-start(f32[2,512]{1,0:T(2,128)} %param.41) | copy-start | bytes 12292
  13.2 34.8 %copy-start.8 = (f32[2,512]{1,0:T(2,128)S(1)}, f32[2,512]{1,0:T(2,128)}, u32[]{:S(2)}) copy-start(f32[2,512]{1,0:T(2,128)} %param.42) | copy-start | bytes 12292
  43.9 7.5 %copy-start.3 = (bf16[1,4,1,9,12,512]{5,1,4,3,2,0:T(4,128)(2,1)S(1)}, bf16[1,4,1,9,12,512]{5,1,4,3,2,0:T(4,128)(2,1)}, u32[]{:S(2)}) copy-start(bf16[1,4,1,9,12,512]{5,1,4,3,2,0:T(4,128)(2,1)} %param.49) | copy-start | bytes 1327108
  43.9 8.4 %copy-start.5 = (f32[1,3,512]{2,0,1:T(1,128)S(1)}, f32[1,3,512]{2,0,1:T(1,128)}, u32[]{:S(2)}) copy-start(f32[1,3,512]{2,0,1:T(1,128)} %param.46) | copy-start | bytes 18436
  43.9 8.4 %copy-start.6 = (f32[1,3,512]{2,0,1:T(1,128)S(1)}, f32[1,3,512]{2,0,1:T(1,128)}, u32[]{:S(2)}) copy-start(f32[1,3,512]{2,0,1:T(1,128)} %param.45) | copy-start | bytes 18436
  43.9 262.7 %reduce-scatter.2.cloned.1.call-start = ((), (), s32[]{:S(2)}) async-start(), calls=%async_computation.2 | async-start | bytes 6488064 | tf_op jit(solution)/shard_map/reduce_scatter | solution.py:835
  204.0 1.0 copy-start.1
  249.4 54.3 %copy-start.13 = (f32[2,2,512]{2,1,0:T(2,128)S(1)}, f32[2,2,512]{2,1,0:T(2,128)}, u32[]{:S(2)}) copy-start(f32[2,2,512]{2,1,0:T(2,128)} %param.43) | copy-start | bytes 24580
  249.4 54.3 %copy-start.14 = (f32[2,2,512]{2,1,0:T(2,128)S(1)}, f32[2,2,512]{2,1,0:T(2,128)}, u32[]{:S(2)}) copy-start(f32[2,2,512]{2,1,0:T(2,128)} %param.44) | copy-start | bytes 24580
  249.4 56.2 %copy-start.9 = (f32[8,512]{1,0:T(8,128)S(1)}, f32[8,512]{1,0:T(8,128)}, u32[]{:S(2)}) copy-start(f32[8,512]{1,0:T(8,128)} %get-tuple-element.129) | copy-start | bytes 49156
  249.4 56.6 %copy-start.11 = (f32[1,3,2,512]{3,2,1,0:T(2,128)S(1)}, f32[1,3,2,512]{3,2,1,0:T(2,128)}, u32[]{:S(2)}) copy-start(f32[1,3,2,512]{3,2,1,0:T(2,128)} %param.47) | copy-start | bytes 36868
  249.4 56.6 %copy-start.12 = (f32[1,3,2,512]{3,2,1,0:T(2,128)S(1)}, f32[1,3,2,512]{3,2,1,0:T(2,128)}, u32[]{:S(2)}) copy-start(f32[1,3,2,512]{3,2,1,0:T(2,128)} %param.48) | copy-start | bytes 36868
  358.0 62.0 %copy-start = (f32[432,512]{1,0:T(8,128)S(1)}, f32[432,512]{1,0:T(8,128)}, u32[]{:S(2)}) copy-start(f32[432,512]{1,0:T(8,128)} %get-tuple-element.109) | copy-start | bytes 2654212
Sparse Core Ops, SparseCore 0:
  44.0 61.6 all-gather.1
  204.1 74.9 reduce-scatter.1
